TPU v7x, 32 devices: a whole 2x2x4 slice. The times are simulated.
32 devices in a mesh: dp: 16 (over z, x, core), col: 2 (over y).
Axes of the slice: x: 2, y: 2, z: 4, core: 2. Of those that a mesh axis runs over, the one named last changes fastest.
Arguments:
- tokens: bfloat16 [2048, 2048], P('dp'), may hold values from -6 to 6
- routes: int32 [2048, 8], P('dp'), may hold values from 0 to 31, all different within a row; in each aligned block of 128 rows (0 to 127, 128 to 255, ...) at most 48 rows name the same one
- probs: float32 [2048, 8], P('dp'), may hold values from 0.1 to 1
- w_gate: bfloat16 [32, 2048, 768], P('dp', None, 'col'), may hold values from -0.125 to 0.125
- w_up: bfloat16 [32, 2048, 768], P('dp', None, 'col'), may hold values from -0.125 to 0.125
- w_down: bfloat16 [32, 768, 2048], P('dp', 'col'), may hold values from -0.21875 to 0.21875
- cotangent: bfloat16 [2048, 2048], P('dp', 'col'), may hold values from -6 to 6
Outputs:
- mixed: bfloat16 [2048, 2048], P('dp', 'col')
- grad_tokens: bfloat16 [2048, 2048], P('dp', 'col')
- grad_probs: float32 [2048, 8], P('dp')
- grad_gate: bfloat16 [32, 2048, 768], P('dp', None, 'col')
- grad_up: bfloat16 [32, 2048, 768], P('dp', None, 'col')
- grad_down: bfloat16 [32, 768, 2048], P('dp', 'col')
Inputs may be any that keep to these rules, and one draw needn't show every extreme that they name: `routes`: each token names 8 different experts. Among the 128 tokens of one index of dp, no expert is named by more than 48 of them, a bound that some block reaches.
All inputs are finite; a program needn't handle non-finite values.
Results may differ from a plain program's by a relative error of at most 0.0064.
Values may be sent and summed in bfloat16 or wider, within the bound.
No kernel may reach another device: no remote copies, remote signals or barrier semaphores. Data moves between devices by JAX's collectives and lax.ppermute only.
A program may use at most 192 MiB of HBM per device.

v0:
```python
import functools

import jax
import jax.numpy as jnp
from jax import lax
from jax.experimental import pallas as pl
from jax.experimental.pallas import tpu as pltpu
from jax.sharding import PartitionSpec as P

BF = jnp.bfloat16
F32 = jnp.float32


def dot(a, b, dims):
    return lax.dot_general(a, b, ((dims[:1], dims[1:]), ((), ())), preferred_element_type=F32)


def begin(src, dst, sem, into):
    copy = pltpu.make_async_copy(src, dst, sem)
    copy.start()
    into.append(copy)


def rounds_kernel(cap, count, at_ref, *refs):
    groups = [refs[8 * i:8 * i + 8] for i in range(count)]
    blocks = [group[b] for group in groups for b in range(4)]
    others = [group[4 + b].at[b % 2 if group[4 + b].shape[0] == 2 else 0] for group in groups for b in range(4)]
    (wg, wu, wd, xs, cs, hs, keep, send, gp,
     x, c, tab, wgu, wdv, xp, cp, hp, row,
     sem_x, sem_c, sem_t, sem_w, sem_o) = refs[8 * count:]
    rows = blocks[0].shape[0]
    pairs = 2 * count
    local, width, hid = wg.shape
    half = width // 2
    outk, outs = x, c
    wide = tab.shape[1]
    col = at_ref[0]
    first = at_ref[1]
    mine = pl.multiple_of(col * half, half)
    theirs = pl.multiple_of((1 - col) * half, half)
    held = 4 * count
    x_copies, c_copies, t_copies, w_copies, o_copies = [], [], [], [], []

    for b, piece in enumerate(blocks):
        begin(piece.at[:, pl.ds(width + half, wide)], tab.at[pl.ds(b * rows, rows), :], sem_t.at[b], t_copies)
    for b, piece in enumerate(blocks):
        for y in range(2):
            begin(piece.at[:, pl.ds(y * half, half)], x.at[y * held + b], sem_x.at[y * held + b], x_copies)
    for e in range(local):
        begin(wg.at[e], wgu.at[e, :, pl.ds(0, hid)], sem_w.at[3 * e], w_copies)
        begin(wu.at[e], wgu.at[e, :, pl.ds(hid, hid)], sem_w.at[3 * e + 1], w_copies)
    for b, piece in enumerate(blocks):
        begin(piece.at[:, pl.ds(width, half)], c.at[col * held + b], sem_c.at[b], c_copies)
        begin(others[b], c.at[(1 - col) * held + b], sem_c.at[held + b], c_copies)
    for e in range(local):
        begin(wd.at[e], wdv.at[e], sem_w.at[3 * e + 2], w_copies)

    two = 2 * rows
    chunk = 2 * cap
    slots = local * chunk
    r_id = lax.broadcasted_iota(jnp.int32, (two, two), 0)
    c_id = lax.broadcasted_iota(jnp.int32, (two, two), 1)
    lower = ((c_id < r_id) & ((c_id < rows) == (r_id < rows))).astype(BF)
    lane = lax.broadcasted_iota(jnp.int32, (two, wide), 1)
    slot_id = lax.broadcasted_iota(jnp.int32, (two, slots), 1)
    base = jnp.where(lax.broadcasted_iota(jnp.int32, (two, 1), 0) < rows, 0, cap)
    s_lane = lax.broadcasted_iota(jnp.int32, (slots, wide), 1)
    s_row = lax.broadcasted_iota(jnp.int32, (slots, wide), 0)
    s_expert = first + s_row // chunk
    for copy in t_copies:
        copy.wait()
    picks, weights = [], []
    for k in range(pairs):
        values = tab[pl.ds(k * two, two), :]
        routed = values.astype(F32) > 0
        before = dot(lower, jnp.where(routed, 1.0, 0.0).astype(BF), (1, 0))
        pick = jnp.zeros((two, slots), F32)
        for e in range(local):
            here = (lane == first + e) & routed
            rank = jnp.sum(jnp.where(here, before + 1.0, 0.0), axis=1, keepdims=True).astype(jnp.int32)
            target = jnp.where(rank > 0, rank - 1 + e * chunk + base, -1)
            pick = pick + jnp.where(slot_id == target, 1.0, 0.0)
        pick = pick.astype(BF)
        picked = dot(pick, values, (0, 0))
        chosen = (s_lane == s_expert) | (s_lane == s_expert + wide // 2)
        picks.append(pick)
        weights.append(jnp.sum(jnp.where(chosen, picked, 0.0), axis=1, keepdims=True))

    def gather(src, dst):
        for k in range(pairs):
            for y in range(2):
                part = dot(picks[k], src[pl.ds(y * held + 2 * k, 2)].reshape(two, half), (0, 0)).astype(BF)
                for e in range(local):
                    dst[e, pl.ds(k * chunk, chunk), pl.ds(y * half, half)] = part[e * chunk:(e + 1) * chunk]

    for copy in x_copies:
        copy.wait()
    gather(x, xp)
    begin(xp, xs, sem_o.at[0], o_copies)
    acts = []
    for e in range(local):
        w_copies[2 * e].wait()
        w_copies[2 * e + 1].wait()
        acts.append(dot(xp[e], wgu[e], (1, 0)))
    for copy in c_copies:
        copy.wait()
    gather(c, cp)
    begin(cp, cs, sem_o.at[1], o_copies)
    prods = []
    for e in range(local):
        w_copies[2 * local + e].wait()
        q = dot(cp[e], wdv[e], (1, 1))
        g, u = acts[e][:, :hid], acts[e][:, hid:]
        p = jnp.concatenate([w[e * chunk:(e + 1) * chunk] for w in weights], axis=0)
        s = 1.0 / (1.0 + jnp.exp(-g))
        silu = g * s
        hidden = (silu * u).astype(BF).astype(F32)
        prods.append(jnp.sum(hidden * q, axis=1, keepdims=True))
        dh = p * q
        hp[e, :, :hid] = (p * hidden).astype(BF)
        hp[e, :, hid:2 * hid] = (dh * u * s * (1.0 + g * (1.0 - s))).astype(BF)
        hp[e, :, 2 * hid:] = (dh * silu).astype(BF)
    begin(hp, hs, sem_o.at[2], o_copies)
    for e in range(local):
        out = dot(hp[e, :, :hid], wdv[e], (1, 0)).astype(BF)
        for k in range(pairs):
            row[k, pl.ds(e * chunk, chunk), :] = out[k * chunk:(k + 1) * chunk]
    for k in range(pairs):
        for y, at in enumerate((mine, theirs)):
            part = dot(picks[k], row[k, :, pl.ds(at, half)], (1, 0)).astype(BF)
            for b in range(2):
                (outk, outs)[k % 2][(y * 2 + b) * count + k // 2] = part[b * rows:(b + 1) * rows]
    for k in range(2):
        half_out = pl.ds(0, 4 * count)
        begin((outk, outs)[k].at[half_out], (keep, send)[k].at[half_out], sem_o.at[3 + k], o_copies)
    for e in range(local):
        out = dot(hp[e, :, hid:], wgu[e], (1, 1)).astype(BF)
        for k in range(pairs):
            row[k, pl.ds(e * chunk, chunk), :] = out[k * chunk:(k + 1) * chunk]
    for k in (*range(1, pairs, 2), *range(0, pairs, 2)):
        for y, at in enumerate((mine, theirs)):
            part = dot(picks[k], row[k, :, pl.ds(at, half)], (1, 0)).astype(BF)
            for b in range(2):
                (outk, outs)[k % 2][(4 + b * 2 + y) * count + k // 2] = part[b * rows:(b + 1) * rows]
        for b in range(4):
            slot = (4 + b) * count + k // 2
            begin((outk, outs)[k % 2].at[slot], (keep, send)[k % 2].at[slot], sem_o.at[5 + 4 * k + b], o_copies)
    for k in range(pairs):
        prod = jnp.concatenate([v[k * chunk:(k + 1) * chunk] for v in prods], axis=0)
        high = prod.astype(BF).astype(F32)
        spread = (jnp.where(s_lane == s_row // chunk, high, 0.0)
                  + jnp.where(s_lane == s_row // chunk + wide // 2, prod - high, 0.0)).astype(BF)
        both = dot(picks[k], spread, (1, 0)).T
        gp[:, pl.ds(k * two, two)] = both[:8] + both[wide // 2:wide // 2 + 8]
    for copy in o_copies:
        copy.wait()


def rounds(at, pieces, cap, wg, wu, wd):
    count = len(pieces) // 8
    rows = pieces[0].shape[0]
    local, width, hid = wg.shape
    half = width // 2
    n = count * 4 * rows
    wide = pieces[0].shape[1] - width - half
    packed = count * 4 * cap
    anyspec = pl.BlockSpec(memory_space=pl.ANY)
    vspec = pl.BlockSpec(memory_space=pltpu.VMEM)
    return pl.pallas_call(
        functools.partial(rounds_kernel, cap, count),
        in_specs=[pl.BlockSpec(memory_space=pltpu.SMEM)] + [anyspec] * (8 * count + 3),
        out_specs=[anyspec] * 5 + [vspec],
        out_shape=[
            jax.ShapeDtypeStruct((local, packed, width), BF),
            jax.ShapeDtypeStruct((local, packed, width), BF),
            jax.ShapeDtypeStruct((local, packed, 3 * hid), BF),
            jax.ShapeDtypeStruct((8 * count, rows, half), BF),
            jax.ShapeDtypeStruct((8 * count, rows, half), BF),
            jax.ShapeDtypeStruct((8, n), F32),
        ],
        scratch_shapes=[
            pltpu.VMEM((8 * count, rows, half), BF),
            pltpu.VMEM((8 * count, rows, half), BF),
            pltpu.VMEM((n, wide), BF),
            pltpu.VMEM((local, width, 2 * hid), BF),
            pltpu.VMEM((local, hid, width), BF),
            pltpu.VMEM((local, packed, width), BF),
            pltpu.VMEM((local, packed, width), BF),
            pltpu.VMEM((local, packed, 3 * hid), BF),
            pltpu.VMEM((2 * count, local * 2 * cap, width), BF),
            pltpu.SemaphoreType.DMA((8 * count,)),
            pltpu.SemaphoreType.DMA((8 * count,)),
            pltpu.SemaphoreType.DMA((4 * count,)),
            pltpu.SemaphoreType.DMA((3 * local,)),
            pltpu.SemaphoreType.DMA((5 + 8 * count,)),
        ],
        compiler_params=pltpu.CompilerParams(vmem_limit_bytes=44 * 1024 * 1024),
        cost_estimate=pl.CostEstimate(
            flops=12 * local * packed * width * hid, bytes_accessed=2 * (3 * local * hid * width + 6 * n * width),
            transcendentals=local * packed * hid),
        name="moe_rounds",
    )(at, *pieces, wg, wu, wd)


def weight_kernel(rounds, off, outs_n, *refs):
    acts, hs = refs[:rounds], refs[rounds:2 * rounds]
    outs = refs[2 * rounds:2 * rounds + outs_n]
    a, h = refs[2 * rounds + outs_n:2 * rounds + outs_n + 2]
    stage = refs[2 * rounds + outs_n + 2:2 * rounds + 2 * outs_n + 2]
    sem_a, sem_h, sem_o = refs[2 * rounds + 2 * outs_n + 2:]
    local, total, width = a.shape
    packed = total // rounds
    cols = h.shape[2]
    hid = cols // outs_n
    copies, o_copies = [], []
    for e in range(local):
        mine = []
        for r in range(rounds):
            begin(hs[r].at[e, :, pl.ds(off, cols)], h.at[e, pl.ds(r * packed, packed), :], sem_h.at[e, r], mine)
            begin(acts[r].at[e], a.at[e, pl.ds(r * packed, packed), :], sem_a.at[e, r], mine)
        copies.append(mine)
    step = 512
    for e in range(local):
        for copy in copies[e]:
            copy.wait()
        for j in range(width // step):
            block = pl.ds(j * step, step)
            if outs_n == 2:
                grad = dot(a[e, :, block], h[e], (0, 0)).astype(BF)
                for i in range(outs_n):
                    stage[i][e, block, :] = grad[:, i * hid:(i + 1) * hid]
                    begin(stage[i].at[e, block], outs[i].at[e, block], sem_o.at[e, j, i], o_copies)
            else:
                stage[0][e, :, block] = dot(h[e], a[e, :, block], (0, 0)).astype(BF)
                begin(stage[0].at[e, :, block], outs[0].at[e, :, block], sem_o.at[e, j, 0], o_copies)
    for copy in o_copies:
        copy.wait()


def weight_grads(acts, hs, off, cols, outs_n, shape, name):
    local, packed, width = acts[0].shape
    rounds = len(acts)
    anyspec = pl.BlockSpec(memory_space=pl.ANY)
    return pl.pallas_call(
        functools.partial(weight_kernel, rounds, off, outs_n),
        in_specs=[anyspec] * (2 * rounds),
        out_specs=[anyspec] * outs_n,
        out_shape=[jax.ShapeDtypeStruct(shape, BF)] * outs_n,
        scratch_shapes=[
            pltpu.VMEM((local, rounds * packed, width), BF),
            pltpu.VMEM((local, rounds * packed, cols), BF),
            *[pltpu.VMEM(shape, BF)] * outs_n,
            pltpu.SemaphoreType.DMA((local, rounds)),
            pltpu.SemaphoreType.DMA((local, rounds)),
            pltpu.SemaphoreType.DMA((local, width // 512, outs_n)),
        ],
        compiler_params=pltpu.CompilerParams(vmem_limit_bytes=22 * 1024 * 1024),
        cost_estimate=pl.CostEstimate(
            flops=2 * local * rounds * packed * width * cols,
            bytes_accessed=2 * local * (rounds * packed * (width + cols) + width * cols), transcendentals=0),
        name=name,
    )(*acts, *hs)


def dense_probs(routes, probs, experts):
    onehot = routes[:, :, None] == jnp.arange(experts, dtype=jnp.int32)
    return jnp.sum(jnp.where(onehot, probs[:, :, None], 0.0), axis=1), onehot


def add(*terms):
    return functools.reduce(lambda a, b: a + b, [t.astype(F32) for t in terms])


sync = lax.optimization_barrier


def add16(*terms):
    return add(*terms).astype(BF)


def body16(tokens, routes, probs, w_gate, w_up, w_down, cotangent):
    rows, width = tokens.shape
    half = width // 2
    local, _, hid = w_gate.shape
    owners = lax.axis_size("dp")
    experts = local * owners
    place = lax.axis_index("dp")
    col = lax.axis_index("col")
    z = place // 4
    middle = (z == 1) | (z == 2)

    def permute(pairs):
        return lambda v: lax.ppermute(v, "dp", pairs)

    over_core = permute([(i, i ^ 1) for i in range(16)])
    over_x = permute([(i, i ^ 2) for i in range(16)])
    over_z = permute([(i, i ^ 4) for i in range(16)])
    across = permute([(4 + j, 8 + j) for j in range(4)] + [(8 + j, 4 + j) for j in range(4)])
    outward = permute([(4 + j, j) for j in range(4)] + [(8 + j, 12 + j) for j in range(4)])
    leap = permute([(4 * a + j, 4 * b + j) for a, b in ((0, 1), (3, 2), (1, 3), (2, 0)) for j in range(4)])
    end_to_end = permute([(j, 12 + j) for j in range(4)] + [(12 + j, j) for j in range(4)])

    def over_y(v):
        return lax.ppermute(v, "col", [(0, 1), (1, 0)])

    table, onehot = dense_probs(routes, probs, experts)
    high = table.astype(BF)
    low = (table - high.astype(F32)).astype(BF)
    gap = jnp.zeros((rows, 64 - experts), BF)
    first = jnp.concatenate([tokens, cotangent, high, gap, low, gap], axis=1)

    def pair(own, other):
        return jnp.stack([own[:, width:width + half], other[:, width:width + half]])

    cap = 3 * rows * routes.shape[1] // (2 * experts)
    at = jnp.stack([col, place * local]).astype(jnp.int32)

    def run(*pieces):
        return rounds(at, pieces, cap, w_gate, w_up, w_down)

    def stage_one(keep, got):
        return over_y(add16(keep[4:8], got[4:8])), over_x(add16(keep[12:16], got[12:16]))

    def stage_two(keep, got, m_got, g_got):
        return (over_x(add16(keep[2:4], got[2:4], m_got[2:4])),
                over_y(add16(keep[10:12], got[10:12], g_got[2:4])))

    def layer_sum(keep, got, one, two, r):
        return jnp.stack([add(keep[r], got[r], one[0][r], two[0][r]),
                          add(keep[8 + r], got[8 + r], one[1][r], two[1][r])])

    l0 = first
    l1, b1, x0 = over_z(l0), across(l0), over_x(l0)
    l0, l1, b1, x0 = sync((l0, l1, b1, x0))

    c1, b2, x1, y0 = across(l1), outward(b1), over_x(l1), over_y(pair(l0, x0))
    k0, kx0 = over_core(l0), over_core(x0)
    l0, l1, b1, b2, c1, x0, x1, y0 = sync((l0, l1, b1, b2, c1, x0, x1, y0))

    l2 = jnp.where(middle, c1, b2)
    c2, x2, y1 = outward(c1), over_x(l2), over_y(pair(l1, x1))
    k1, kx1, ky0 = over_core(l1), over_core(x1), over_core(y0)
    l2, c2, x2, y1 = sync((l2, c2, x2, y1))

    l3 = jnp.where(middle, b1, c2)
    x3, y2, y3 = over_x(l3), over_y(pair(l2, x2)), over_y(l3[None, :, width:width + half])
    ky1 = over_core(y1)
    k2, kx2, k3 = over_core(l2), over_core(x2), over_core(l3)
    xs_a, cs_a, hs_a, keep_a, send_a, gp_a = run(
        l0, x0, k0, kx0, y0, y0, ky0, ky0, l1, x1, k1, kx1, y1, y1, ky1, ky1)
    l2, x2, l3, x3, y2, y3, k2, kx2, k3, keep_a, send_a = sync(
        (l2, x2, l3, x3, y2, y3, k2, kx2, k3, keep_a, send_a))

    yx3 = over_y(x3[None, :, width:width + half])
    ky2, kx3, ky3 = over_core(y2), over_core(x3), over_core(y3)
    got_a = over_core(send_a)
    yx3, ky2, kx3, ky3, keep_a, got_a = sync((yx3, ky2, kx3, ky3, keep_a, got_a))

    kyx3 = over_core(yx3)
    one_a = stage_one(keep_a, got_a)
    xs_b, cs_b, hs_b, keep_b, send_b, gp_b = run(
        l2, x2, k2, kx2, y2, y2, ky2, ky2, l3, x3, k3, kx3, y3, yx3, ky3, kyx3)
    one_a, keep_b, send_b = sync((one_a, keep_b, send_b))

    got_b = over_core(send_b)
    two_a = stage_two(keep_a, got_a, *one_a)
    got_b, two_a = sync((got_b, two_a))

    one_b = stage_one(keep_b, got_b)
    from1 = over_z(layer_sum(keep_a, got_a, one_a, two_a, 1).astype(BF))
    grad_gate, grad_up = weight_grads([xs_a, xs_b], [hs_a, hs_b], hid, 2 * hid, 2, w_gate.shape, "grad_in")
    gps = jnp.concatenate([gp_a[:local], gp_b[:local]], axis=1).reshape(local, 4, 4, rows)
    gps = gps[:, :, jnp.array([0, 2, 1, 3])].reshape(local, owners, rows).transpose(1, 0, 2)
    gps = gps[jnp.arange(owners) ^ place]
    one_b, from1, grad_gate, grad_up, gps = sync((one_b, from1, grad_gate, grad_up, gps))

    two_b = stage_two(keep_b, got_b, *one_b)
    back = lax.all_to_all(gps, "dp", 0, 0, tiled=True)
    two_b, back = sync((two_b, back))

    sum2, sum3 = layer_sum(keep_b, got_b, one_b, two_b, 0).astype(BF), layer_sum(keep_b, got_b, one_b, two_b, 1)
    step, ends = leap(sum2), end_to_end(sum3.astype(BF))
    (grad_down,) = weight_grads([cs_a, cs_b], [hs_a, hs_b], 0, hid, 1, w_down.shape, "grad_down")
    other_back = over_y(back)
    sum3, step, ends, grad_down, other_back = sync((sum3, step, ends, grad_down, other_back))

    inner = across(add16(sum3, step))
    result = add16(layer_sum(keep_a, got_a, one_a, two_a, 0), from1, jnp.where(middle, inner, add16(step, ends)))

    back = (back + other_back).reshape(experts, rows).T
    grad_probs = jnp.sum(jnp.where(onehot, back[:, None, :], 0.0), axis=2)
    return result[0], result[1], grad_probs, grad_gate, grad_up, grad_down


def body_any(tokens, routes, probs, w_gate, w_up, w_down, cotangent):
    rows, width = tokens.shape
    half = width // 2
    local, _, hid = w_gate.shape
    owners = lax.axis_size("dp")
    experts = local * owners
    parts = max(1, rows * owners // 2048)
    step = rows // parts
    table, onehot = dense_probs(routes, probs, experts)
    arrived = lax.all_to_all(table.reshape(rows, owners, local).transpose(1, 0, 2), "dp", 0, 0, tiled=True)
    def one_part(grads, inputs):
        own_x, own_c, own_p = inputs
        x = lax.all_gather(own_x, "dp", axis=0, tiled=True)
        c = lax.all_gather(lax.all_gather(own_c, "dp", axis=0, tiled=True), "col", axis=1, tiled=True)
        p = own_p.reshape(owners * step, local).T[:, :, None]
        gate = jnp.einsum("td,ldh->lth", x, w_gate, preferred_element_type=F32)
        up = jnp.einsum("td,ldh->lth", x, w_up, preferred_element_type=F32)
        q = jnp.einsum("td,lhd->lth", c, w_down, preferred_element_type=F32)
        s = jax.nn.sigmoid(gate)
        silu = gate * s
        hidden = (silu * up).astype(BF).astype(F32)
        dh = p * q
        hp = (p * hidden).astype(BF)
        dg = (dh * up * s * (1.0 + gate * (1.0 - s))).astype(BF)
        du = (dh * silu).astype(BF)
        m = jnp.einsum("lth,lhd->td", hp, w_down, preferred_element_type=F32).astype(BF)
        g = (jnp.einsum("lth,ldh->td", dg, w_gate, preferred_element_type=F32)
             + jnp.einsum("lth,ldh->td", du, w_up, preferred_element_type=F32)).astype(BF)
        sums = []
        for part in (m, g):
            part = lax.psum_scatter(part, "dp", scatter_dimension=0, tiled=True)
            sums.append(lax.psum_scatter(part, "col", scatter_dimension=1, tiled=True))
        new = (jnp.einsum("td,lth->ldh", x, dg, preferred_element_type=F32),
               jnp.einsum("td,lth->ldh", x, du, preferred_element_type=F32),
               jnp.einsum("lth,td->lhd", hp, c, preferred_element_type=F32))
        grads = tuple(a + b for a, b in zip(grads, new))
        return grads, (*sums, jnp.sum(hidden * q, axis=2))

    zeros = tuple(jnp.zeros(w.shape, F32) for w in (w_gate, w_up, w_down))
    arrived = arrived.reshape(owners, parts, step, local).transpose(1, 0, 2, 3)
    grads, (mixed, grad_tokens, gps) = lax.scan(
        one_part, zeros,
        (tokens.reshape(parts, step, width), cotangent.reshape(parts, step, half), arrived))
    back = gps.reshape(parts, local, owners, step).transpose(2, 0, 3, 1).reshape(owners, rows, local)
    back = lax.all_to_all(back, "dp", 0, 0, tiled=True)
    back = lax.psum(back.transpose(1, 0, 2).reshape(rows, experts), "col")
    grad_probs = jnp.sum(jnp.where(onehot, back[:, None, :], 0.0), axis=2)
    return (mixed.reshape(rows, half), grad_tokens.reshape(rows, half), grad_probs,
            *(v.astype(BF) for v in grads))


def solution(mesh):
    body = body16 if mesh.shape["dp"] == 16 and mesh.shape["col"] == 2 else body_any
    return jax.shard_map(
        body,
        mesh=mesh,
        in_specs=(
            P("dp", None),
            P("dp", None),
            P("dp", None),
            P("dp", None, "col"),
            P("dp", None, "col"),
            P("dp", "col", None),
            P("dp", "col"),
        ),
        out_specs=(
            P("dp", "col"),
            P("dp", "col"),
            P("dp", None),
            P("dp", None, "col"),
            P("dp", None, "col"),
            P("dp", "col", None),
        ),
        check_vma=False,
    )
```

profile of v0, /device:TPU:8, one launch (start us, length us, event | category | flops | bytes accessed | tf_op | source)
XLA Modules:
  0.0 248.4 jit_solution(17201315076609649189)
XLA Ops:
  3.0 5.0 %collective-permute-start.1 = (bf16[128,3200]{1,0:T(8,128)(2,1)S(1)}, bf16[128,3200]{1,0:T(8,128)(2,1)}, u32[]{:S(2)}, u32[]{:S(2)}) collective-permute-start(bf16[128,3200]{1,0:T(8,128)(2,1)S(1)} %concatenate.6.refs_0_), channel_id=1, source_target_pairs={{8,16},{10,18},{12,20},{14,22},{16,8},{18,10},{20,12},{22,14},{9,1... | collective-permute-start | bytes 2457608 | tf_op jit(solution)/shard_map/ppermute | solution.py:293
  9.6 13.4 %collective-permute-done.refs_8_ = bf16[128,3200]{1,0:T(8,128)(2,1)S(1)} collective-permute-done((bf16[128,3200]{1,0:T(8,128)(2,1)S(1)}, bf16[128,3200]{1,0:T(8,128)(2,1)S(1)}, u32[]{:S(2)}, u32[]{:S(2)}) %collective-permute-start) | collective-permute-done | bytes 819232 | tf_op jit(solution)/shard_map/ppermute | solution.py:293
  22.9 3.1 %collective-permute-done.1 = bf16[128,3200]{1,0:T(8,128)(2,1)} collective-permute-done((bf16[128,3200]{1,0:T(8,128)(2,1)S(1)}, bf16[128,3200]{1,0:T(8,128)(2,1)}, u32[]{:S(2)}, u32[]{:S(2)}) %collective-permute-start.1) | collective-permute-done | bytes 819232 | tf_op jit(solution)/shard_map/ppermute | solution.py:293
  27.5 2.2 collective-permute-start.4
  31.3 2.2 collective-permute-start.3
  35.2 10.5 %collective-permute-done.6.refs_4_.refs_5_ = bf16[2,128,1024]{2,1,0:T(8,128)(2,1)S(1)} collective-permute-done((bf16[2,128,1024]{2,1,0:T(8,128)(2,1)S(1)}, bf16[2,128,1024]{2,1,0:T(8,128)(2,1)S(1)}, u32[]{:S(2)}, u32[]{:S(2)}) %collective-permute-start.6) | collective-permute-done | bytes 524320 | tf_op jit(solution)/shard_map/ppermute | solution.py:304
  45.7 2.4 collective-permute-done.4
  49.3 5.0 %collective-permute-start.7 = (bf16[128,3200]{1,0:T(8,128)(2,1)}, bf16[128,3200]{1,0:T(8,128)(2,1)}, u32[]{:S(2)}, u32[]{:S(2)}) collective-permute-start(bf16[128,3200]{1,0:T(8,128)(2,1)} %collective-permute-done.4), channel_id=1, source_target_pairs={{8,0},{10,2},{12,4},{14,6},{16,24},{18,26},{20,28},{22,30},{9,1},{... | collective-permute-start | bytes 2457608 | tf_op jit(solution)/shard_map/ppermute | solution.py:293
  59.1 9.1 %collective-permute-done.9.refs_12_.refs_13_ = bf16[2,128,1024]{2,1,0:T(8,128)(2,1)} collective-permute-done((bf16[2,128,1024]{2,1,0:T(8,128)(2,1)}, bf16[2,128,1024]{2,1,0:T(8,128)(2,1)}, u32[]{:S(2)}, u32[]{:S(2)}) %collective-permute-start.9) | collective-permute-done | bytes 524320 | tf_op jit(solution)/shard_map/ppermute | solution.py:304
  68.2 4.9 %collective-permute-done.8.refs_1_ = bf16[128,3200]{1,0:T(8,128)(2,1)S(1)} collective-permute-done((bf16[128,3200]{1,0:T(8,128)(2,1)S(1)}, bf16[128,3200]{1,0:T(8,128)(2,1)S(1)}, u32[]{:S(2)}, u32[]{:S(2)}) %collective-permute-start.8) | collective-permute-done | bytes 819232 | tf_op jit(solution)/shard_map/ppermute | solution.py:293
  77.7 5.4 %collective-permute-done.12.refs_12_ = bf16[1,128,1024]{2,1,0:T(8,128)(2,1)S(1)} collective-permute-done((bf16[1,128,1024]{2,1,0:T(8,128)(2,1)S(1)}, bf16[1,128,1024]{2,1,0:T(8,128)(2,1)S(1)}, u32[]{:S(2)}, u32[]{:S(2)}) %collective-permute-start.12) | collective-permute-done | bytes 262176 | tf_op jit(solution)/shard_map/ppermute | solution.py:304
  84.8 20.1 %moe_rounds.2 = (bf16[2,384,2048]{2,1,0:T(8,128)(2,1)}, bf16[2,384,2048]{2,1,0:T(8,128)(2,1)}, bf16[2,384,1152]{2,1,0:T(8,128)(2,1)}, bf16[16,128,1024]{2,1,0:T(...) custom-call(s32[2]{0:T(128)S(1)} %pad_add_fusion.at_ref, bf16[128,3200]{1,0:T(8,128)(2,1)S(1)} %concatenate.6.refs_0_, ...), custom_call_target="tpu_custom_call" | custom-call | flops 7247757312 | bytes 34603008 | tf_op jit(solution)/shard_map/moe_rounds/pallas_call | solution.py:169
  106.3 8.0 %collective-permute-done.22.refs_13_ = bf16[1,128,1024]{2,1,0:T(8,128)(2,1)S(1)} collective-permute-done((bf16[1,128,1024]{2,1,0:T(8,128)(2,1)S(1)}, bf16[1,128,1024]{2,1,0:T(8,128)(2,1)S(1)}, u32[]{:S(2)}, u32[]{:S(2)}) %collective-permute-start.22) | collective-permute-done | bytes 262176 | tf_op jit(solution)/shard_map/ppermute | solution.py:304
  114.7 2.5 %add_convert_fusion.2 = (bf16[4,128,1024]{2,1,0:T(8,128)(2,1)S(1)}, bf16[4,128,1024]{2,1,0:T(8,128)(2,1)S(1)}) fusion(bf16[16,128,1024]{2,1,0:T(8,128)(2,1)S(1)} %collective-permute-done.26, bf16[16,128,1024]{2,1,0:T(8,128)(2,1)} %get-tuple-element.97), kind=kLoop, calls=%fused_computation.4 | loop fusion | flops 4194304 | bytes 6291456 | tf_op jit(solution)/shard_map/convert_element_type | solution.py:278
  119.8 19.6 %moe_rounds.3 = (bf16[2,384,2048]{2,1,0:T(8,128)(2,1)}, bf16[2,384,2048]{2,1,0:T(8,128)(2,1)}, bf16[2,384,1152]{2,1,0:T(8,128)(2,1)}, bf16[16,128,1024]{2,1,0:T(...) custom-call(s32[2]{0:T(128)S(1)} %pad_add_fusion.at_ref, ...), custom_call_target="tpu_custom_call" | custom-call | flops 7247757312 | bytes 34603008 | tf_op jit(solution)/shard_map/moe_rounds/pallas_call | solution.py:169
  139.5 3.1 %collective-permute-done.27 = bf16[4,128,1024]{2,1,0:T(8,128)(2,1)S(1)} collective-permute-done((bf16[4,128,1024]{2,1,0:T(8,128)(2,1)S(1)}, bf16[4,128,1024]{2,1,0:T(8,128)(2,1)S(1)}, u32[]{:S(2)}, u32[]{:S(2)}) %collective-permute-start.27) | collective-permute-done | bytes 1048608 | tf_op jit(solution)/shard_map/ppermute | solution.py:304
  142.9 1.7 add_convert_fusion.6
  147.9 11.1 %collective-permute-done.31 = bf16[2,128,1024]{2,1,0:T(8,128)(2,1)S(1)} collective-permute-done((bf16[2,128,1024]{2,1,0:T(8,128)(2,1)S(1)}, bf16[2,128,1024]{2,1,0:T(8,128)(2,1)S(1)}, u32[]{:S(2)}, u32[]{:S(2)}) %collective-permute-start.31) | collective-permute-done | bytes 524320 | tf_op jit(solution)/shard_map/ppermute | solution.py:293
  159.2 2.7 %add_convert_fusion = (bf16[4,128,1024]{2,1,0:T(8,128)(2,1)}, bf16[4,128,1024]{2,1,0:T(8,128)(2,1)}) fusion(bf16[16,128,1024]{2,1,0:T(8,128)(2,1)S(1)} %collective-permute-done.30, bf16[16,128,1024]{2,1,0:T(8,128)(2,1)S(1)} %copy-done.13), kind=kLoop, calls=%fused_computation.2 | loop fusion | flops 4194304 | bytes 6291456 | tf_op jit(solution)/shard_map/convert_element_type | solution.py:278
  164.9 3.0 %add_convert_fusion.11 = (bf16[1,128,1024]{2,1,0:T(8,128)(2,1)S(1)}, f32[1,128,1024]{2,1,0:T(8,128)}, f32[1,128,1024]{2,1,0:T(8,128)}, bf16[1,128,1024]{2,1,0:T(8,128)(2,1)S(1)}) fusion(bf16[2,128,1024]{2,1,0:T(8,128)(2,1)S(1)} %collective-permute-done.31, bf16[4,128,1024]{2,1,0:T(8,128)(2,1)} %copy-done.19, ...), kind=kLoop, calls=%fused_computation.31 | loop fusion | flops 3932160 | bytes 5767168 | tf_op jit(solution)/shard_map/convert.2
  174.3 1.9 copy-done.10
  176.1 1.9 copy-done.11
  178.0 7.0 %grad_in.1 = (bf16[2,2048,384]{2,1,0:T(8,128)(2,1)}, bf16[2,2048,384]{2,1,0:T(8,128)(2,1)}) custom-call(bf16[2,384,2048]{2,1,0:T(8,128)(2,1)S(1)} %copy-done.10, bf16[2,384,2048]{2,1,0:T(8,128)(2,1)S(1)} %copy-done.11, bf16[2,384,1152]{2,1,0:T(8,128)(2,1)S(1)} %copy-done.2, bf16[2,384,1152]{2,1,0:T(8,128)(2,1)S(1)} %copy-done.3), custom_call_target="tpu_custom_call" | custom-call | flops 4831838208 | bytes 14942208 | tf_op jit(solution)/shard_map/grad_in/pallas_call | solution.py:244
  188.0 1.8 add_convert_fusion.4
  191.8 10.4 %all_to_all.5 = f32[16,2,128]{2,1,0:T(2,128)S(1)} all-to-all(f32[16,2,128]{2,1,0:T(2,128)S(1)} %gather_fusion.1), channel_id=1, replica_groups=mesh['dp'=16,'col'=2] {'dp'}, dimensions={0} | all-to-all | bytes 32768 | tf_op jit(solution)/shard_map/all_to_all | solution.py:378
  203.1 2.5 add_convert_fusion.9
  206.4 2.5 collective-permute-start.38
  208.9 4.5 %grad_down.1 = bf16[2,384,2048]{2,1,0:T(8,128)(2,1)} custom-call(bf16[2,384,2048]{2,1,0:T(8,128)(2,1)S(1)} %copy-done, bf16[2,384,2048]{2,1,0:T(8,128)(2,1)S(1)} %copy-done.1, bf16[2,384,1152]{2,1,0:T(8,128)(2,1)S(1)} %copy-done.2, bf16[2,384,1152]{2,1,0:T(8,128)(2,1)S(1)} %copy-done.3), custom_call_target="tpu_custom_call" | custom-call | flops 2415919104 | bytes 10616832 | tf_op jit(solution)/shard_map/grad_down/pallas_call | solution.py:244
  215.0 2.1 collective-permute-done.40
  217.2 13.9 %collective-permute-done.38 = bf16[2,128,1024]{2,1,0:T(8,128)(2,1)S(1)} collective-permute-done((bf16[2,128,1024]{2,1,0:T(8,128)(2,1)S(1)}, bf16[2,128,1024]{2,1,0:T(8,128)(2,1)S(1)}, u32[]{:S(2)}, u32[]{:S(2)}) %collective-permute-start.38) | collective-permute-done | bytes 524320 | tf_op jit(solution)/shard_map/ppermute | solution.py:293
  231.2 3.0 %collective-permute-start.41 = (bf16[2,128,1024]{2,1,0:T(8,128)(2,1)S(1)}, bf16[2,128,1024]{2,1,0:T(8,128)(2,1)S(1)}, u32[]{:S(2)}, u32[]{:S(2)}) collective-permute-start(bf16[2,128,1024]{2,1,0:T(8,128)(2,1)S(1)} %fusion), channel_id=1, source_target_pairs={{8,16},{10,18},{12,20},{14,22},{16,8},{18,10},{20,12},{22,14},{9,1... | collective-permute-start | bytes 1572872 | tf_op jit(solution)/shard_map/ppermute | solution.py:293
  234.8 11.0 %collective-permute-done.41 = bf16[2,128,1024]{2,1,0:T(8,128)(2,1)S(1)} collective-permute-done((bf16[2,128,1024]{2,1,0:T(8,128)(2,1)S(1)}, bf16[2,128,1024]{2,1,0:T(8,128)(2,1)S(1)}, u32[]{:S(2)}, u32[]{:S(2)}) %collective-permute-start.41) | collective-permute-done | bytes 524320 | tf_op jit(solution)/shard_map/ppermute | solution.py:293
  (148 shorter events, 49.7 us)
Async XLA Ops:
  2.9 20.0 %collective-permute-start = (bf16[128,3200]{1,0:T(8,128)(2,1)S(1)}, bf16[128,3200]{1,0:T(8,128)(2,1)S(1)}, u32[]{:S(2)}, u32[]{:S(2)}) collective-permute-start(bf16[128,3200]{1,0:T(8,128)(2,1)S(1)} %concatenate.6.refs_0_), channel_id=1, source_target_pairs={{0,8},{2,10},{4,12},{6,14},{8,0},{10,2},{12,4},{14,6},{16,24},{18,... | collective-permute-start | bytes 2457608 | tf_op jit(solution)/shard_map/ppermute | solution.py:293
  3.0 23.1 %collective-permute-start.1 = (bf16[128,3200]{1,0:T(8,128)(2,1)S(1)}, bf16[128,3200]{1,0:T(8,128)(2,1)}, u32[]{:S(2)}, u32[]{:S(2)}) collective-permute-start(bf16[128,3200]{1,0:T(8,128)(2,1)S(1)} %concatenate.6.refs_0_), channel_id=1, source_target_pairs={{8,16},{10,18},{12,20},{14,22},{16,8},{18,10},{20,12},{22,14},{9,1... | collective-permute-start | bytes 2457608 | tf_op jit(solution)/shard_map/ppermute | solution.py:293
  8.0 19.5 %collective-permute-start.2 = (bf16[128,3200]{1,0:T(8,128)(2,1)S(1)}, bf16[128,3200]{1,0:T(8,128)(2,1)S(1)}, u32[]{:S(2)}, u32[]{:S(2)}) collective-permute-start(bf16[128,3200]{1,0:T(8,128)(2,1)S(1)} %concatenate.6.refs_0_), channel_id=1, source_target_pairs={{0,4},{2,6},{4,0},{6,2},{8,12},{10,14},{12,8},{14,10},{16,20},{18,... | collective-permute-start | bytes 2457608 | tf_op jit(solution)/shard_map/ppermute | solution.py:293
  27.5 20.6 %collective-permute-start.4 = (bf16[128,3200]{1,0:T(8,128)(2,1)S(1)}, bf16[128,3200]{1,0:T(8,128)(2,1)}, u32[]{:S(2)}, u32[]{:S(2)}) collective-permute-start(bf16[128,3200]{1,0:T(8,128)(2,1)S(1)} %collective-permute-done.refs_8_), channel_id=1, source_target_pairs={{8,16},{10,18},{12,20},{14,22},{16,8},{18,10},{20,12},{22,14},{9,1... | collective-permute-start | bytes 2457608 | tf_op jit(solution)/shard_map/ppermute | solution.py:293
  29.7 18.7 %collective-permute-start.5 = (bf16[128,3200]{1,0:T(8,128)(2,1)S(1)}, bf16[128,3200]{1,0:T(8,128)(2,1)S(1)}, u32[]{:S(2)}, u32[]{:S(2)}) collective-permute-start(bf16[128,3200]{1,0:T(8,128)(2,1)S(1)} %collective-permute-done.refs_8_), channel_id=1, source_target_pairs={{0,4},{2,6},{4,0},{6,2},{8,12},{10,14},{12,8},{14,10},{16,20},{18,... | collective-permute-start | bytes 2457608 | tf_op jit(solution)/shard_map/ppermute | solution.py:293
  31.3 17.7 %collective-permute-start.3 = (bf16[128,3200]{1,0:T(8,128)(2,1)}, bf16[128,3200]{1,0:T(8,128)(2,1)}, u32[]{:S(2)}, u32[]{:S(2)}) collective-permute-start(bf16[128,3200]{1,0:T(8,128)(2,1)} %collective-permute-done.1), channel_id=1, source_target_pairs={{8,0},{10,2},{12,4},{14,6},{16,24},{18,26},{20,28},{22,30},{9,1},{... | collective-permute-start | bytes 2457608 | tf_op jit(solution)/shard_map/ppermute | solution.py:293
  33.6 12.1 %collective-permute-start.6 = (bf16[2,128,1024]{2,1,0:T(8,128)(2,1)S(1)}, bf16[2,128,1024]{2,1,0:T(8,128)(2,1)S(1)}, u32[]{:S(2)}, u32[]{:S(2)}) collective-permute-start(bf16[2,128,1024]{2,1,0:T(8,128)(2,1)S(1)} %pad_maximum_fusion.1), channel_id=1, source_target_pairs={{0,1},{1,0},{2,3},{3,2},{4,5},{5,4},{6,7},{7,6},{8,9},{9,8},{10,11... | collective-permute-start | bytes 1572872 | tf_op jit(solution)/shard_map/ppermute | solution.py:304
  49.3 23.8 %collective-permute-start.7 = (bf16[128,3200]{1,0:T(8,128)(2,1)}, bf16[128,3200]{1,0:T(8,128)(2,1)}, u32[]{:S(2)}, u32[]{:S(2)}) collective-permute-start(bf16[128,3200]{1,0:T(8,128)(2,1)} %collective-permute-done.4), channel_id=1, source_target_pairs={{8,0},{10,2},{12,4},{14,6},{16,24},{18,26},{20,28},{22,30},{9,1},{... | collective-permute-start | bytes 2457608 | tf_op jit(solution)/shard_map/ppermute | solution.py:293
  55.6 17.5 %collective-permute-start.8 = (bf16[128,3200]{1,0:T(8,128)(2,1)S(1)}, bf16[128,3200]{1,0:T(8,128)(2,1)S(1)}, u32[]{:S(2)}, u32[]{:S(2)}) collective-permute-start(bf16[128,3200]{1,0:T(8,128)(2,1)S(1)} %broadcast_select_fusion.1.refs_0_), channel_id=1, source_target_pairs={{0,4},{2,6},{4,0},{6,2},{8,12},{10,14},{12,8},{14,10},{16,20},{18,... | collective-permute-start | bytes 2457608 | tf_op jit(solution)/shard_map/ppermute | solution.py:293
  57.0 11.1 %collective-permute-start.9 = (bf16[2,128,1024]{2,1,0:T(8,128)(2,1)}, bf16[2,128,1024]{2,1,0:T(8,128)(2,1)}, u32[]{:S(2)}, u32[]{:S(2)}) collective-permute-start(bf16[2,128,1024]{2,1,0:T(8,128)(2,1)} %pad_maximum_fusion.2), channel_id=1, source_target_pairs={{0,1},{1,0},{2,3},{3,2},{4,5},{5,4},{6,7},{7,6},{8,9},{9,8},{10,11... | collective-permute-start | bytes 1572872 | tf_op jit(solution)/shard_map/ppermute | solution.py:304
  58.6 16.3 %collective-permute-start.16 = (bf16[128,3200]{1,0:T(8,128)(2,1)S(1)}, bf16[128,3200]{1,0:T(8,128)(2,1)S(1)}, u32[]{:S(2)}, u32[]{:S(2)}) collective-permute-start(bf16[128,3200]{1,0:T(8,128)(2,1)S(1)} %concatenate.6.refs_0_), channel_id=1, source_target_pairs={{0,2},{2,0},{4,6},{6,4},{8,10},{10,8},{12,14},{14,12},{16,18},{18,... | collective-permute-start | bytes 2457608 | tf_op jit(solution)/shard_map/ppermute | solution.py:293
  58.6 17.9 %collective-permute-start.17 = (bf16[128,3200]{1,0:T(8,128)(2,1)}, bf16[128,3200]{1,0:T(8,128)(2,1)S(1)}, u32[]{:S(2)}, u32[]{:S(2)}) collective-permute-start(bf16[128,3200]{1,0:T(8,128)(2,1)} %copy-done.6), channel_id=1, source_target_pairs={{0,2},{2,0},{4,6},{6,4},{8,10},{10,8},{12,14},{14,12},{16,18},{18,... | collective-permute-start | bytes 2457608 | tf_op jit(solution)/shard_map/ppermute | solution.py:293
  76.5 28.3 %collective-permute-start.10 = (bf16[128,3200]{1,0:T(8,128)(2,1)S(1)}, bf16[128,3200]{1,0:T(8,128)(2,1)S(1)}, u32[]{:S(2)}, u32[]{:S(2)}) collective-permute-start(bf16[128,3200]{1,0:T(8,128)(2,1)S(1)} %broadcast_select_fusion.refs_8_), channel_id=1, source_target_pairs={{0,4},{2,6},{4,0},{6,2},{8,12},{10,14},{12,8},{14,10},{16,20},{18,... | collective-permute-start | bytes 2457608 | tf_op jit(solution)/shard_map/ppermute | solution.py:293
  77.2 27.8 %collective-permute-start.15 = (bf16[128,3200]{1,0:T(8,128)(2,1)S(1)}, bf16[128,3200]{1,0:T(8,128)(2,1)S(1)}, u32[]{:S(2)}, u32[]{:S(2)}) collective-permute-start(bf16[128,3200]{1,0:T(8,128)(2,1)S(1)} %broadcast_select_fusion.refs_8_), channel_id=1, source_target_pairs={{0,2},{2,0},{4,6},{6,4},{8,10},{10,8},{12,14},{14,12},{16,18},{18,... | collective-permute-start | bytes 2457608 | tf_op jit(solution)/shard_map/ppermute | solution.py:293
  77.4 27.6 %collective-permute-start.14 = (bf16[128,3200]{1,0:T(8,128)(2,1)S(1)}, bf16[128,3200]{1,0:T(8,128)(2,1)S(1)}, u32[]{:S(2)}, u32[]{:S(2)}) collective-permute-start(bf16[128,3200]{1,0:T(8,128)(2,1)S(1)} %collective-permute-done.8.refs_1_), channel_id=1, source_target_pairs={{0,2},{2,0},{4,6},{6,4},{8,10},{10,8},{12,14},{14,12},{16,18},{18,... | collective-permute-start | bytes 2457608 | tf_op jit(solution)/shard_map/ppermute | solution.py:293
  83.1 21.8 %collective-permute-start.13 = (bf16[128,3200]{1,0:T(8,128)(2,1)S(1)}, bf16[128,3200]{1,0:T(8,128)(2,1)S(1)}, u32[]{:S(2)}, u32[]{:S(2)}) collective-permute-start(bf16[128,3200]{1,0:T(8,128)(2,1)S(1)} %broadcast_select_fusion.1.refs_0_), channel_id=1, source_target_pairs={{0,2},{2,0},{4,6},{6,4},{8,10},{10,8},{12,14},{14,12},{16,18},{18,... | collective-permute-start | bytes 2457608 | tf_op jit(solution)/shard_map/ppermute | solution.py:293
  83.2 21.7 %collective-permute-start.11 = (bf16[2,128,1024]{2,1,0:T(8,128)(2,1)S(1)}, bf16[2,128,1024]{2,1,0:T(8,128)(2,1)S(1)}, u32[]{:S(2)}, u32[]{:S(2)}) collective-permute-start(bf16[2,128,1024]{2,1,0:T(8,128)(2,1)S(1)} %pad_maximum_fusion.3), channel_id=1, source_target_pairs={{0,1},{1,0},{2,3},{3,2},{4,5},{5,4},{6,7},{7,6},{8,9},{9,8},{10,11... | collective-permute-start | bytes 1572872 | tf_op jit(solution)/shard_map/ppermute | solution.py:304
  104.9 9.7 %collective-permute-start.26 = (bf16[16,128,1024]{2,1,0:T(8,128)(2,1)}, bf16[16,128,1024]{2,1,0:T(8,128)(2,1)S(1)}, u32[]{:S(2)}, u32[]{:S(2)}) collective-permute-start(bf16[16,128,1024]{2,1,0:T(8,128)(2,1)} %get-tuple-element.96), channel_id=1, source_target_pairs={{0,2},{2,0},{4,6},{6,4},{8,10},{10,8},{12,14},{14,12},{16,18},{18,... | collective-permute-start | bytes 12582920 | tf_op jit(solution)/shard_map/ppermute | solution.py:293
  105.2 9.1 %collective-permute-start.24 = (bf16[128,3200]{1,0:T(8,128)(2,1)S(1)}, bf16[128,3200]{1,0:T(8,128)(2,1)S(1)}, u32[]{:S(2)}, u32[]{:S(2)}) collective-permute-start(bf16[128,3200]{1,0:T(8,128)(2,1)S(1)} %collective-permute-done.10.refs_9_), channel_id=1, source_target_pairs={{0,2},{2,0},{4,6},{6,4},{8,10},{10,8},{12,14},{14,12},{16,18},{18,... | collective-permute-start | bytes 2457608 | tf_op jit(solution)/shard_map/ppermute | solution.py:293
  117.2 25.4 %collective-permute-start.27 = (bf16[4,128,1024]{2,1,0:T(8,128)(2,1)S(1)}, bf16[4,128,1024]{2,1,0:T(8,128)(2,1)S(1)}, u32[]{:S(2)}, u32[]{:S(2)}) collective-permute-start(bf16[4,128,1024]{2,1,0:T(8,128)(2,1)S(1)} %get-tuple-element.161), channel_id=1, source_target_pairs={{0,1},{1,0},{2,3},{3,2},{4,5},{5,4},{6,7},{7,6},{8,9},{9,8},{10,11... | collective-permute-start | bytes 3145736 | tf_op jit(solution)/shard_map/ppermute | solution.py:304
  117.8 25.1 %collective-permute-start.28 = (bf16[4,128,1024]{2,1,0:T(8,128)(2,1)S(1)}, bf16[4,128,1024]{2,1,0:T(8,128)(2,1)}, u32[]{:S(2)}, u32[]{:S(2)}) collective-permute-start(bf16[4,128,1024]{2,1,0:T(8,128)(2,1)S(1)} %get-tuple-element.160), channel_id=1, source_target_pairs={{0,4},{2,6},{4,0},{6,2},{8,12},{10,14},{12,8},{14,10},{16,20},{18,... | collective-permute-start | bytes 3145736 | tf_op jit(solution)/shard_map/ppermute | solution.py:293
  142.9 16.4 %collective-permute-start.30 = (bf16[16,128,1024]{2,1,0:T(8,128)(2,1)}, bf16[16,128,1024]{2,1,0:T(8,128)(2,1)S(1)}, u32[]{:S(2)}, u32[]{:S(2)}) collective-permute-start(bf16[16,128,1024]{2,1,0:T(8,128)(2,1)} %get-tuple-element.112), channel_id=1, source_target_pairs={{0,2},{2,0},{4,6},{6,4},{8,10},{10,8},{12,14},{14,12},{16,18},{18,... | collective-permute-start | bytes 12582920 | tf_op jit(solution)/shard_map/ppermute | solution.py:293
  144.6 14.4 %collective-permute-start.31 = (bf16[2,128,1024]{2,1,0:T(8,128)(2,1)S(1)}, bf16[2,128,1024]{2,1,0:T(8,128)(2,1)S(1)}, u32[]{:S(2)}, u32[]{:S(2)}) collective-permute-start(bf16[2,128,1024]{2,1,0:T(8,128)(2,1)S(1)} %get-tuple-element.159), channel_id=1, source_target_pairs={{0,4},{2,6},{4,0},{6,2},{8,12},{10,14},{12,8},{14,10},{16,20},{18,... | collective-permute-start | bytes 1572872 | tf_op jit(solution)/shard_map/ppermute | solution.py:293
  145.2 14.0 %collective-permute-start.32 = (bf16[2,128,1024]{2,1,0:T(8,128)(2,1)S(1)}, bf16[2,128,1024]{2,1,0:T(8,128)(2,1)S(1)}, u32[]{:S(2)}, u32[]{:S(2)}) collective-permute-start(bf16[2,128,1024]{2,1,0:T(8,128)(2,1)S(1)} %get-tuple-element.158), channel_id=1, source_target_pairs={{0,1},{1,0},{2,3},{3,2},{4,5},{5,4},{6,7},{7,6},{8,9},{9,8},{10,11... | collective-permute-start | bytes 1572872 | tf_op jit(solution)/shard_map/ppermute | solution.py:304
  161.9 24.8 %collective-permute-start.33 = (bf16[4,128,1024]{2,1,0:T(8,128)(2,1)}, bf16[4,128,1024]{2,1,0:T(8,128)(2,1)}, u32[]{:S(2)}, u32[]{:S(2)}) collective-permute-start(bf16[4,128,1024]{2,1,0:T(8,128)(2,1)} %get-tuple-element.157), channel_id=1, source_target_pairs={{0,1},{1,0},{2,3},{3,2},{4,5},{5,4},{6,7},{7,6},{8,9},{9,8},{10,11... | collective-permute-start | bytes 3145736 | tf_op jit(solution)/shard_map/ppermute | solution.py:304
  163.4 24.6 %collective-permute-start.34 = (bf16[4,128,1024]{2,1,0:T(8,128)(2,1)}, bf16[4,128,1024]{2,1,0:T(8,128)(2,1)}, u32[]{:S(2)}, u32[]{:S(2)}) collective-permute-start(bf16[4,128,1024]{2,1,0:T(8,128)(2,1)} %get-tuple-element.156), channel_id=1, source_target_pairs={{0,4},{2,6},{4,0},{6,2},{8,12},{10,14},{12,8},{14,10},{16,20},{18,... | collective-permute-start | bytes 3145736 | tf_op jit(solution)/shard_map/ppermute | solution.py:293
  168.8 16.2 %collective-permute-start.35 = (bf16[2,128,1024]{2,1,0:T(8,128)(2,1)}, bf16[2,128,1024]{2,1,0:T(8,128)(2,1)}, u32[]{:S(2)}, u32[]{:S(2)}) collective-permute-start(bf16[2,128,1024]{2,1,0:T(8,128)(2,1)} %pad_maximum_fusion.4), channel_id=1, source_target_pairs={{0,8},{2,10},{4,12},{6,14},{8,0},{10,2},{12,4},{14,6},{16,24},{18,... | collective-permute-start | bytes 1572872 | tf_op jit(solution)/shard_map/ppermute | solution.py:293
  189.8 12.4 %collective-permute-start.36 = (bf16[2,128,1024]{2,1,0:T(8,128)(2,1)S(1)}, bf16[2,128,1024]{2,1,0:T(8,128)(2,1)S(1)}, u32[]{:S(2)}, u32[]{:S(2)}) collective-permute-start(bf16[2,128,1024]{2,1,0:T(8,128)(2,1)S(1)} %get-tuple-element.153), channel_id=1, source_target_pairs={{0,4},{2,6},{4,0},{6,2},{8,12},{10,14},{12,8},{14,10},{16,20},{18,... | collective-permute-start | bytes 1572872 | tf_op jit(solution)/shard_map/ppermute | solution.py:293
  191.3 11.8 %collective-permute-start.37 = (bf16[2,128,1024]{2,1,0:T(8,128)(2,1)S(1)}, bf16[2,128,1024]{2,1,0:T(8,128)(2,1)S(1)}, u32[]{:S(2)}, u32[]{:S(2)}) collective-permute-start(bf16[2,128,1024]{2,1,0:T(8,128)(2,1)S(1)} %get-tuple-element.152), channel_id=1, source_target_pairs={{0,1},{1,0},{2,3},{3,2},{4,5},{5,4},{6,7},{7,6},{8,9},{9,8},{10,11... | collective-permute-start | bytes 1572872 | tf_op jit(solution)/shard_map/ppermute | solution.py:304
  205.6 11.5 %collective-permute-start.39 = (bf16[2,128,1024]{2,1,0:T(8,128)(2,1)S(1)}, bf16[2,128,1024]{2,1,0:T(8,128)(2,1)S(1)}, u32[]{:S(2)}, u32[]{:S(2)}) collective-permute-start(bf16[2,128,1024]{2,1,0:T(8,128)(2,1)S(1)} %fusion.6), channel_id=1, source_target_pairs={{0,24},{2,26},{4,28},{6,30},{24,0},{26,2},{28,4},{30,6},{1,25},{3,... | collective-permute-start | bytes 1572872 | tf_op jit(solution)/shard_map/ppermute | solution.py:293
  206.4 24.6 %collective-permute-start.38 = (bf16[2,128,1024]{2,1,0:T(8,128)(2,1)S(1)}, bf16[2,128,1024]{2,1,0:T(8,128)(2,1)S(1)}, u32[]{:S(2)}, u32[]{:S(2)}) collective-permute-start(bf16[2,128,1024]{2,1,0:T(8,128)(2,1)S(1)} %pad_maximum_fusion.5), channel_id=1, source_target_pairs={{0,8},{2,10},{4,12},{6,14},{24,16},{26,18},{28,20},{30,22},{8,24},... | collective-permute-start | bytes 1572872 | tf_op jit(solution)/shard_map/ppermute | solution.py:293
  231.2 14.7 %collective-permute-start.41 = (bf16[2,128,1024]{2,1,0:T(8,128)(2,1)S(1)}, bf16[2,128,1024]{2,1,0:T(8,128)(2,1)S(1)}, u32[]{:S(2)}, u32[]{:S(2)}) collective-permute-start(bf16[2,128,1024]{2,1,0:T(8,128)(2,1)S(1)} %fusion), channel_id=1, source_target_pairs={{8,16},{10,18},{12,20},{14,22},{16,8},{18,10},{20,12},{22,14},{9,1... | collective-permute-start | bytes 1572872 | tf_op jit(solution)/shard_map/ppermute | solution.py:293
  (32 other events, 375.5 us)
where the time goes:
time: 252 us; the launch traced here: 248 us
  waiting for transfers between devices  107 us (42%)
  Pallas kernels  51.1 us (20%)
  starting transfers between devices  44 us (17%)
  other arithmetic  23 us (9%)
  local copies, waits for them, and re-layouts  12 us (5%)
  blocking collectives  10.4 us (4%)
    ppermute x32, waiting for transfers between devices, permute(): return lambda v: lax.ppermute(v, 'dp', pairs)  65.6 us
    ppermute x10, waiting for transfers between devices, over_y(): return lax.ppermute(v, 'col', [(0, 1), (1, 0)])  41 us
    pallas_call x2, Pallas kernels, rounds(): pl.pallas_call(functools.partial(rounds_kernel, cap, count), in_specs=[pl...  39.7 us
    ppermute x32, starting transfers between devices, permute(): return lambda v: lax.ppermute(v, 'dp', pairs)  31.5 us
    ppermute x10, starting transfers between devices, over_y(): return lax.ppermute(v, 'col', [(0, 1), (1, 0)])  12.5 us
    pallas_call x2, Pallas kernels, weight_grads(): pl.pallas_call(functools.partial(weight_kernel, rounds, off, outs_n), in_...  11.4 us
    all_to_all x1, blocking collectives, body16(): back = lax.all_to_all(gps, 'dp', 0, 0, tiled=True)  10.4 us
    convert_element_type x6, other arithmetic, add16(): return add(*terms).astype(BF)  10.3 us
  transfers between devices with their start and end apart: 42, of which 23 were waited for; matrix products, arithmetic and copies ran while one was open for 7% of the time, Pallas kernels for 21%

commit v1 on v0

--- a/solution.py
+++ b/solution.py
@@ -21,10 +21,11 @@
     into.append(copy)
 
 
-def rounds_kernel(cap, count, at_ref, *refs):
-    groups = [refs[8 * i:8 * i + 8] for i in range(count)]
+def rounds_kernel(cap, count, index, at_ref, *refs):
+    views = [ref if i is None else ref.at[i] for ref, i in zip(refs, index)]
+    groups = [views[8 * i:8 * i + 8] for i in range(count)]
     blocks = [group[b] for group in groups for b in range(4)]
-    others = [group[4 + b].at[b % 2 if group[4 + b].shape[0] == 2 else 0] for group in groups for b in range(4)]
+    others = [group[4 + b] for group in groups for b in range(4)]
     (wg, wu, wd, xs, cs, hs, keep, send, gp,
      x, c, tab, wgu, wdv, xp, cp, hp, row,
      sem_x, sem_c, sem_t, sem_w, sem_o) = refs[8 * count:]
@@ -158,6 +159,7 @@
 
 def rounds(at, pieces, cap, wg, wu, wd):
     count = len(pieces) // 8
+    pieces, index = zip(*(p if isinstance(p, tuple) else (p, None) for p in pieces))
     rows = pieces[0].shape[0]
     local, width, hid = wg.shape
     half = width // 2
@@ -167,7 +169,7 @@
     anyspec = pl.BlockSpec(memory_space=pl.ANY)
     vspec = pl.BlockSpec(memory_space=pltpu.VMEM)
     return pl.pallas_call(
-        functools.partial(rounds_kernel, cap, count),
+        functools.partial(rounds_kernel, cap, count, index),
         in_specs=[pl.BlockSpec(memory_space=pltpu.SMEM)] + [anyspec] * (8 * count + 3),
         out_specs=[anyspec] * 5 + [vspec],
         out_shape=[
@@ -309,8 +311,8 @@
     gap = jnp.zeros((rows, 64 - experts), BF)
     first = jnp.concatenate([tokens, cotangent, high, gap, low, gap], axis=1)
 
-    def pair(own, other):
-        return jnp.stack([own[:, width:width + half], other[:, width:width + half]])
+    def cotangents(*sources):
+        return jnp.stack([v[:, width:width + half] for v in sources])
 
     cap = 3 * rows * routes.shape[1] // (2 * experts)
     at = jnp.stack([col, place * local]).astype(jnp.int32)
@@ -333,59 +335,74 @@
     l1, b1, x0 = over_z(l0), across(l0), over_x(l0)
     l0, l1, b1, x0 = sync((l0, l1, b1, x0))
 
-    c1, b2, x1, y0 = across(l1), outward(b1), over_x(l1), over_y(pair(l0, x0))
+    c1, b2, x1, y0 = across(l1), outward(b1), over_x(l1), over_y(cotangents(l0, x0))
     k0, kx0 = over_core(l0), over_core(x0)
     l0, l1, b1, b2, c1, x0, x1, y0 = sync((l0, l1, b1, b2, c1, x0, x1, y0))
 
     l2 = jnp.where(middle, c1, b2)
-    c2, x2, y1 = outward(c1), over_x(l2), over_y(pair(l1, x1))
+    c2, x2, y1 = outward(c1), over_x(l2), over_y(cotangents(l1, x1))
     k1, kx1, ky0 = over_core(l1), over_core(x1), over_core(y0)
     l2, c2, x2, y1 = sync((l2, c2, x2, y1))
 
     l3 = jnp.where(middle, b1, c2)
-    x3, y2, y3 = over_x(l3), over_y(pair(l2, x2)), over_y(l3[None, :, width:width + half])
+    x3, y2 = over_x(l3), over_y(cotangents(l2, x2, l3))
     ky1 = over_core(y1)
     k2, kx2, k3 = over_core(l2), over_core(x2), over_core(l3)
     xs_a, cs_a, hs_a, keep_a, send_a, gp_a = run(
-        l0, x0, k0, kx0, y0, y0, ky0, ky0, l1, x1, k1, kx1, y1, y1, ky1, ky1)
-    l2, x2, l3, x3, y2, y3, k2, kx2, k3, keep_a, send_a = sync(
-        (l2, x2, l3, x3, y2, y3, k2, kx2, k3, keep_a, send_a))
-
-    yx3 = over_y(x3[None, :, width:width + half])
-    ky2, kx3, ky3 = over_core(y2), over_core(x3), over_core(y3)
+        l0, x0, k0, kx0, (y0, 0), (y0, 1), (ky0, 0), (ky0, 1),
+        l1, x1, k1, kx1, (y1, 0), (y1, 1), (ky1, 0), (ky1, 1))
+    l2, x2, l3, x3, y2, k2, kx2, k3, keep_a, send_a = sync(
+        (l2, x2, l3, x3, y2, k2, kx2, k3, keep_a, send_a))
+
+    yx3, ky2, kx3 = over_y(cotangents(x3)), over_core(y2), over_core(x3)
     got_a = over_core(send_a)
-    yx3, ky2, kx3, ky3, keep_a, got_a = sync((yx3, ky2, kx3, ky3, keep_a, got_a))
+    yx3, ky2, kx3, keep_a, got_a = sync((yx3, ky2, kx3, keep_a, got_a))
 
     kyx3 = over_core(yx3)
     one_a = stage_one(keep_a, got_a)
     xs_b, cs_b, hs_b, keep_b, send_b, gp_b = run(
-        l2, x2, k2, kx2, y2, y2, ky2, ky2, l3, x3, k3, kx3, y3, yx3, ky3, kyx3)
+        l2, x2, k2, kx2, (y2, 0), (y2, 1), (ky2, 0), (ky2, 1),
+        l3, x3, k3, kx3, (y2, 2), (yx3, 0), (ky2, 2), (kyx3, 0))
     one_a, keep_b, send_b = sync((one_a, keep_b, send_b))
 
     got_b = over_core(send_b)
     two_a = stage_two(keep_a, got_a, *one_a)
     got_b, two_a = sync((got_b, two_a))
 
-    one_b = stage_one(keep_b, got_b)
-    from1 = over_z(layer_sum(keep_a, got_a, one_a, two_a, 1).astype(BF))
-    grad_gate, grad_up = weight_grads([xs_a, xs_b], [hs_a, hs_b], hid, 2 * hid, 2, w_gate.shape, "grad_in")
+    def first_sums(i):
+        return over_y(add16(keep_b[4 + i:8:2], got_b[4 + i:8:2])), over_x(add16(keep_b[12 + i:16:2], got_b[12 + i:16:2]))
+
+    def second_sums(i, one):
+        return (over_x(add16(keep_b[2 + i], got_b[2 + i], one[0][1])),
+                over_y(add16(keep_b[10 + i], got_b[10 + i], one[1][1])))
+
+    def whole_sum(i, one, two):
+        return jnp.stack([add16(keep_b[i], got_b[i], one[0][0], two[0]),
+                          add16(keep_b[8 + i], got_b[8 + i], one[1][0], two[1])])
+
+    one_2 = first_sums(0)
     gps = jnp.concatenate([gp_a[:local], gp_b[:local]], axis=1).reshape(local, 4, 4, rows)
     gps = gps[:, :, jnp.array([0, 2, 1, 3])].reshape(local, owners, rows).transpose(1, 0, 2)
     gps = gps[jnp.arange(owners) ^ place]
-    one_b, from1, grad_gate, grad_up, gps = sync((one_b, from1, grad_gate, grad_up, gps))
-
-    two_b = stage_two(keep_b, got_b, *one_b)
+    one_2, gps = sync((one_2, gps))
+
+    one_3, two_2 = first_sums(1), second_sums(0, one_2)
+    from1 = over_z(layer_sum(keep_a, got_a, one_a, two_a, 1).astype(BF))
+    grad_gate, grad_up = weight_grads([xs_a, xs_b], [hs_a, hs_b], hid, 2 * hid, 2, w_gate.shape, "grad_in")
+    one_3, two_2, from1, grad_gate, grad_up = sync((one_3, two_2, from1, grad_gate, grad_up))
+
+    two_3 = second_sums(1, one_3)
+    step = leap(whole_sum(0, one_2, two_2))
     back = lax.all_to_all(gps, "dp", 0, 0, tiled=True)
-    two_b, back = sync((two_b, back))
-
-    sum2, sum3 = layer_sum(keep_b, got_b, one_b, two_b, 0).astype(BF), layer_sum(keep_b, got_b, one_b, two_b, 1)
-    step, ends = leap(sum2), end_to_end(sum3.astype(BF))
+    two_3, step, back = sync((two_3, step, back))
+
+    sum3 = whole_sum(1, one_3, two_3)
+    ends, inner = end_to_end(sum3), across(add16(sum3, step))
+    other_back = over_y(back)
     (grad_down,) = weight_grads([cs_a, cs_b], [hs_a, hs_b], 0, hid, 1, w_down.shape, "grad_down")
-    other_back = over_y(back)
-    sum3, step, ends, grad_down, other_back = sync((sum3, step, ends, grad_down, other_back))
-
-    inner = across(add16(sum3, step))
-    result = add16(layer_sum(keep_a, got_a, one_a, two_a, 0), from1, jnp.where(middle, inner, add16(step, ends)))
+    ends, inner, other_back, grad_down = sync((ends, inner, other_back, grad_down))
+    own = layer_sum(keep_a, got_a, one_a, two_a, 0)
+    result = add16(own, from1, jnp.where(middle, inner, add16(step, ends)))
 
     back = (back + other_back).reshape(experts, rows).T
     grad_probs = jnp.sum(jnp.where(onehot, back[:, None, :], 0.0), axis=2)

time: 252 us -> 240 us (0.952)
  local copies, waits for them, and re-layouts: 12 us -> 5.71 us
  waiting for transfers between devices: 107 us -> 101 us
    ppermute x10 -> x11, waiting for transfers between devices: 41 us -> 37.4 us  [over_y(): return lax.ppermute(v, 'col', [(0, 1), (1, 0)])]
    unnamed x44 -> x38, local copies, waits for them, and re-layouts: 4.12 us -> 1.07 us
    ppermute x32 -> x33, waiting for transfers between devices: 65.6 us -> 63.2 us  [permute(): return lambda v: lax.ppermute(v, 'dp', pairs)]
    convert_element_type x6 -> x7, other arithmetic: 10.3 us -> 12.4 us  [add16(): return add(*terms).astype(BF)]
    another operation x5 -> x8, other arithmetic: 6.45 us -> 7.52 us  [the longest x4 3.35 us: whole_sum(): jnp.stack([add16(keep_b[i], got_b[i], one[0][0], two[0]), add16(keep_b[8...]
    ppermute x10 -> x11, starting transfers between devices: 12.5 us -> 11.8 us  [over_y(): return lax.ppermute(v, 'col', [(0, 1), (1, 0)])]
    ppermute x32 -> x33, starting transfers between devices: 31.5 us -> 31.5 us  [permute(): return lambda v: lax.ppermute(v, 'dp', pairs)]
  transfers between devices with their start and end apart: 42 -> 44, of which waited for: 23 -> 21; matrix products, arithmetic and copies ran while one was open for 7% -> 6% of each run, Pallas kernels for 21% -> 22%
where the time goes in v1:
time: 240 us; the launch traced here: 237 us
  waiting for transfers between devices  101 us (42%)
  Pallas kernels  51.2 us (21%)
  starting transfers between devices  43.3 us (18%)
  other arithmetic  23.9 us (10%)
  blocking collectives  10.7 us (4%)
  local copies, waits for them, and re-layouts  5.71 us (2%)
    ppermute x33, waiting for transfers between devices, permute(): return lambda v: lax.ppermute(v, 'dp', pairs)  63.2 us
    pallas_call x2, Pallas kernels, rounds(): pl.pallas_call(functools.partial(rounds_kernel, cap, count, index), in_sp...  39.7 us
    ppermute x11, waiting for transfers between devices, over_y(): return lax.ppermute(v, 'col', [(0, 1), (1, 0)])  37.4 us
    ppermute x33, starting transfers between devices, permute(): return lambda v: lax.ppermute(v, 'dp', pairs)  31.5 us
    convert_element_type x7, other arithmetic, add16(): return add(*terms).astype(BF)  12.4 us
    ppermute x11, starting transfers between devices, over_y(): return lax.ppermute(v, 'col', [(0, 1), (1, 0)])  11.8 us
    pallas_call x2, Pallas kernels, weight_grads(): pl.pallas_call(functools.partial(weight_kernel, rounds, off, outs_n), in_...  11.4 us
    all_to_all x1, blocking collectives, body16(): back = lax.all_to_all(gps, 'dp', 0, 0, tiled=True)  10.7 us
  transfers between devices with their start and end apart: 44, of which 21 were waited for; matrix products, arithmetic and copies ran while one was open for 6% of the time, Pallas kernels for 22%

profile of v1, /device:TPU:8, one launch (start us, length us, event | category | flops | bytes accessed | tf_op | source)
XLA Modules:
  0.0 236.8 jit_solution(11593916877780155222)
XLA Ops:
  3.0 5.0 %collective-permute-start.1 = (bf16[128,3200]{1,0:T(8,128)(2,1)S(1)}, bf16[128,3200]{1,0:T(8,128)(2,1)}, u32[]{:S(2)}, u32[]{:S(2)}) collective-permute-start(bf16[128,3200]{1,0:T(8,128)(2,1)S(1)} %concatenate.6.refs_0_), channel_id=1, source_target_pairs={{8,16},{10,18},{12,20},{14,22},{16,8},{18,10},{20,12},{22,14},{9,1... | collective-permute-start | bytes 2457608 | tf_op jit(solution)/shard_map/ppermute | solution.py:295
  9.6 13.4 %collective-permute-done.refs_8_ = bf16[128,3200]{1,0:T(8,128)(2,1)S(1)} collective-permute-done((bf16[128,3200]{1,0:T(8,128)(2,1)S(1)}, bf16[128,3200]{1,0:T(8,128)(2,1)S(1)}, u32[]{:S(2)}, u32[]{:S(2)}) %collective-permute-start) | collective-permute-done | bytes 819232 | tf_op jit(solution)/shard_map/ppermute | solution.py:295
  22.9 3.1 %collective-permute-done.1 = bf16[128,3200]{1,0:T(8,128)(2,1)} collective-permute-done((bf16[128,3200]{1,0:T(8,128)(2,1)S(1)}, bf16[128,3200]{1,0:T(8,128)(2,1)}, u32[]{:S(2)}, u32[]{:S(2)}) %collective-permute-start.1) | collective-permute-done | bytes 819232 | tf_op jit(solution)/shard_map/ppermute | solution.py:295
  27.5 2.2 collective-permute-start.4
  31.3 2.2 collective-permute-start.3
  33.6 1.6 collective-permute-start.6
  35.2 10.5 %collective-permute-done.6.refs_4_.refs_5_ = bf16[2,128,1024]{2,1,0:T(8,128)(2,1)S(1)} collective-permute-done((bf16[2,128,1024]{2,1,0:T(8,128)(2,1)S(1)}, bf16[2,128,1024]{2,1,0:T(8,128)(2,1)S(1)}, u32[]{:S(2)}, u32[]{:S(2)}) %collective-permute-start.6) | collective-permute-done | bytes 524320 | tf_op jit(solution)/shard_map/ppermute | solution.py:306
  45.6 2.4 %collective-permute-done.4 = bf16[128,3200]{1,0:T(8,128)(2,1)} collective-permute-done((bf16[128,3200]{1,0:T(8,128)(2,1)S(1)}, bf16[128,3200]{1,0:T(8,128)(2,1)}, u32[]{:S(2)}, u32[]{:S(2)}) %collective-permute-start.4) | collective-permute-done | bytes 819232 | tf_op jit(solution)/shard_map/ppermute | solution.py:295
  49.0 5.3 %collective-permute-start.7 = (bf16[128,3200]{1,0:T(8,128)(2,1)}, bf16[128,3200]{1,0:T(8,128)(2,1)}, u32[]{:S(2)}, u32[]{:S(2)}) collective-permute-start(bf16[128,3200]{1,0:T(8,128)(2,1)} %collective-permute-done.4), channel_id=1, source_target_pairs={{8,0},{10,2},{12,4},{14,6},{16,24},{18,26},{20,28},{22,30},{9,1},{... | collective-permute-start | bytes 2457608 | tf_op jit(solution)/shard_map/ppermute | solution.py:295
  59.1 9.1 %collective-permute-done.9.refs_12_.refs_13_ = bf16[2,128,1024]{2,1,0:T(8,128)(2,1)} collective-permute-done((bf16[2,128,1024]{2,1,0:T(8,128)(2,1)}, bf16[2,128,1024]{2,1,0:T(8,128)(2,1)}, u32[]{:S(2)}, u32[]{:S(2)}) %collective-permute-start.9) | collective-permute-done | bytes 524320 | tf_op jit(solution)/shard_map/ppermute | solution.py:306
  68.2 5.0 %collective-permute-done.8.refs_1_ = bf16[128,3200]{1,0:T(8,128)(2,1)} collective-permute-done((bf16[128,3200]{1,0:T(8,128)(2,1)S(1)}, bf16[128,3200]{1,0:T(8,128)(2,1)}, u32[]{:S(2)}, u32[]{:S(2)}) %collective-permute-start.8) | collective-permute-done | bytes 819232 | tf_op jit(solution)/shard_map/ppermute | solution.py:295
  77.5 1.6 collective-permute-start.11
  79.1 20.1 %moe_rounds.2 = (bf16[2,384,2048]{2,1,0:T(8,128)(2,1)}, bf16[2,384,2048]{2,1,0:T(8,128)(2,1)}, bf16[2,384,1152]{2,1,0:T(8,128)(2,1)}, bf16[16,128,1024]{2,1,0:T(...) custom-call(s32[2]{0:T(128)S(1)} %pad_add_fusion.at_ref, bf16[128,3200]{1,0:T(8,128)(2,1)S(1)} %concatenate.6.refs_0_, ...), custom_call_target="tpu_custom_call" | custom-call | flops 7247757312 | bytes 34603008 | tf_op jit(solution)/shard_map/moe_rounds/pallas_call | solution.py:171
  100.5 8.2 %collective-permute-done.21.refs_13_ = bf16[1,128,1024]{2,1,0:T(8,128)(2,1)S(1)} collective-permute-done((bf16[1,128,1024]{2,1,0:T(8,128)(2,1)S(1)}, bf16[1,128,1024]{2,1,0:T(8,128)(2,1)S(1)}, u32[]{:S(2)}, u32[]{:S(2)}) %collective-permute-start.21) | collective-permute-done | bytes 262176 | tf_op jit(solution)/shard_map/ppermute | solution.py:306
  109.0 4.1 %add_convert_fusion = (bf16[4,128,1024]{2,1,0:T(8,128)(2,1)S(1)}, bf16[4,128,1024]{2,1,0:T(8,128)(2,1)S(1)}) fusion(bf16[16,128,1024]{2,1,0:T(8,128)(2,1)S(1)} %collective-permute-done.24, bf16[16,128,1024]{2,1,0:T(8,128)(2,1)} %get-tuple-element.98), kind=kLoop, calls=%fused_computation.2 | loop fusion | flops 4194304 | bytes 6291456 | tf_op jit(solution)/shard_map/convert_element_type | solution.py:280
  116.7 19.7 %moe_rounds.3 = (bf16[2,384,2048]{2,1,0:T(8,128)(2,1)}, bf16[2,384,2048]{2,1,0:T(8,128)(2,1)}, bf16[2,384,1152]{2,1,0:T(8,128)(2,1)}, bf16[16,128,1024]{2,1,0:T(...) custom-call(s32[2]{0:T(128)S(1)} %pad_add_fusion.at_ref, ...), custom_call_target="tpu_custom_call" | custom-call | flops 7247757312 | bytes 34603008 | tf_op jit(solution)/shard_map/moe_rounds/pallas_call | solution.py:171
  136.4 2.0 collective-permute-done.25
  138.6 2.4 add_convert_fusion.6
  144.0 10.9 %collective-permute-done.29 = bf16[2,128,1024]{2,1,0:T(8,128)(2,1)S(1)} collective-permute-done((bf16[2,128,1024]{2,1,0:T(8,128)(2,1)S(1)}, bf16[2,128,1024]{2,1,0:T(8,128)(2,1)S(1)}, u32[]{:S(2)}, u32[]{:S(2)}) %collective-permute-start.29) | collective-permute-done | bytes 524320 | tf_op jit(solution)/shard_map/ppermute | solution.py:295
  156.1 2.1 add_convert_fusion.2
  162.5 3.2 %add_convert_fusion.11 = (bf16[1,128,1024]{2,1,0:T(8,128)(2,1)S(1)}, f32[1,128,1024]{2,1,0:T(8,128)S(1)}, f32[1,128,1024]{2,1,0:T(8,128)S(1)}, bf16[1,128,1024]{2,1,0:T(8,128)(2,1)S(1)}) fusion(bf16[2,128,1024]{2,1,0:T(8,128)(2,1)} %copy-done.15, bf16[4,128,1024]{2,1,0:T(8,128)(2,1)} %copy-done.13, bf16[16,128,1024]{2,1,0:T(8,128)(2,1)} %copy-done.12, ...), kind=kLoop, calls=%fused_computation.37 | loop fusion | flops 3932160 | bytes 5767168 | tf_op jit(solution)/shard_map/convert
  167.9 6.4 %collective-permute-done.33 = bf16[2,128,1024]{2,1,0:T(8,128)(2,1)} collective-permute-done((bf16[2,128,1024]{2,1,0:T(8,128)(2,1)}, bf16[2,128,1024]{2,1,0:T(8,128)(2,1)}, u32[]{:S(2)}, u32[]{:S(2)}) %collective-permute-start.33) | collective-permute-done | bytes 524320 | tf_op jit(solution)/shard_map/ppermute | solution.py:306
  175.9 1.6 fusion.10
  178.6 7.0 %grad_in.1 = (bf16[2,2048,384]{2,1,0:T(8,128)(2,1)}, bf16[2,2048,384]{2,1,0:T(8,128)(2,1)}) custom-call(bf16[2,384,2048]{2,1,0:T(8,128)(2,1)S(1)} %copy-done.9, bf16[2,384,2048]{2,1,0:T(8,128)(2,1)S(1)} %copy-done.8, bf16[2,384,1152]{2,1,0:T(8,128)(2,1)S(1)} %copy-done.2, bf16[2,384,1152]{2,1,0:T(8,128)(2,1)S(1)} %copy-done.3), custom_call_target="tpu_custom_call" | custom-call | flops 4831838208 | bytes 14942208 | tf_op jit(solution)/shard_map/grad_in/pallas_call | solution.py:246
  187.0 3.3 %collective-permute-done.35 = bf16[128,1024]{1,0:T(8,128)(2,1)S(1)} collective-permute-done((bf16[128,1024]{1,0:T(8,128)(2,1)S(1)}, bf16[128,1024]{1,0:T(8,128)(2,1)S(1)}, u32[]{:S(2)}, u32[]{:S(2)}) %collective-permute-start.35) | collective-permute-done | bytes 262176 | tf_op jit(solution)/shard_map/ppermute | solution.py:295
  190.3 1.7 fusion.14
  192.2 1.6 fusion.12
  195.1 10.7 %all_to_all.5 = f32[16,2,128]{2,1,0:T(2,128)S(1)} all-to-all(f32[16,2,128]{2,1,0:T(2,128)S(1)} %gather_fusion.1), channel_id=1, replica_groups=mesh['dp'=16,'col'=2] {'dp'}, dimensions={0} | all-to-all | bytes 32768 | tf_op jit(solution)/shard_map/all_to_all | solution.py:396
  207.6 2.5 %collective-permute-start.42 = (bf16[2,128,1024]{2,1,0:T(8,128)(2,1)S(1)}, bf16[2,128,1024]{2,1,0:T(8,128)(2,1)S(1)}, u32[]{:S(2)}, u32[]{:S(2)}) collective-permute-start(bf16[2,128,1024]{2,1,0:T(8,128)(2,1)S(1)} %fusion), channel_id=1, source_target_pairs={{8,16},{10,18},{12,20},{14,22},{16,8},{18,10},{20,12},{22,14},{9,1... | collective-permute-start | bytes 1572872 | tf_op jit(solution)/shard_map/ppermute | solution.py:295
  210.8 1.6 collective-permute-start.43
  212.4 4.5 %grad_down.1 = bf16[2,384,2048]{2,1,0:T(8,128)(2,1)} custom-call(bf16[2,384,2048]{2,1,0:T(8,128)(2,1)S(1)} %copy-done, bf16[2,384,2048]{2,1,0:T(8,128)(2,1)S(1)} %copy-done.1, bf16[2,384,1152]{2,1,0:T(8,128)(2,1)S(1)} %copy-done.2, bf16[2,384,1152]{2,1,0:T(8,128)(2,1)S(1)} %copy-done.3), custom_call_target="tpu_custom_call" | custom-call | flops 2415919104 | bytes 10616832 | tf_op jit(solution)/shard_map/grad_down/pallas_call | solution.py:246
  216.9 17.8 %collective-permute-done.42 = bf16[2,128,1024]{2,1,0:T(8,128)(2,1)S(1)} collective-permute-done((bf16[2,128,1024]{2,1,0:T(8,128)(2,1)S(1)}, bf16[2,128,1024]{2,1,0:T(8,128)(2,1)S(1)}, u32[]{:S(2)}, u32[]{:S(2)}) %collective-permute-start.42) | collective-permute-done | bytes 524320 | tf_op jit(solution)/shard_map/ppermute | solution.py:295
  (147 shorter events, 42.8 us)
Async XLA Ops:
  2.9 20.0 %collective-permute-start = (bf16[128,3200]{1,0:T(8,128)(2,1)S(1)}, bf16[128,3200]{1,0:T(8,128)(2,1)S(1)}, u32[]{:S(2)}, u32[]{:S(2)}) collective-permute-start(bf16[128,3200]{1,0:T(8,128)(2,1)S(1)} %concatenate.6.refs_0_), channel_id=1, source_target_pairs={{0,8},{2,10},{4,12},{6,14},{8,0},{10,2},{12,4},{14,6},{16,24},{18,... | collective-permute-start | bytes 2457608 | tf_op jit(solution)/shard_map/ppermute | solution.py:295
  3.0 23.1 %collective-permute-start.1 = (bf16[128,3200]{1,0:T(8,128)(2,1)S(1)}, bf16[128,3200]{1,0:T(8,128)(2,1)}, u32[]{:S(2)}, u32[]{:S(2)}) collective-permute-start(bf16[128,3200]{1,0:T(8,128)(2,1)S(1)} %concatenate.6.refs_0_), channel_id=1, source_target_pairs={{8,16},{10,18},{12,20},{14,22},{16,8},{18,10},{20,12},{22,14},{9,1... | collective-permute-start | bytes 2457608 | tf_op jit(solution)/shard_map/ppermute | solution.py:295
  8.0 19.5 %collective-permute-start.2 = (bf16[128,3200]{1,0:T(8,128)(2,1)S(1)}, bf16[128,3200]{1,0:T(8,128)(2,1)S(1)}, u32[]{:S(2)}, u32[]{:S(2)}) collective-permute-start(bf16[128,3200]{1,0:T(8,128)(2,1)S(1)} %concatenate.6.refs_0_), channel_id=1, source_target_pairs={{0,4},{2,6},{4,0},{6,2},{8,12},{10,14},{12,8},{14,10},{16,20},{18,... | collective-permute-start | bytes 2457608 | tf_op jit(solution)/shard_map/ppermute | solution.py:295
  27.5 20.6 %collective-permute-start.4 = (bf16[128,3200]{1,0:T(8,128)(2,1)S(1)}, bf16[128,3200]{1,0:T(8,128)(2,1)}, u32[]{:S(2)}, u32[]{:S(2)}) collective-permute-start(bf16[128,3200]{1,0:T(8,128)(2,1)S(1)} %collective-permute-done.refs_8_), channel_id=1, source_target_pairs={{8,16},{10,18},{12,20},{14,22},{16,8},{18,10},{20,12},{22,14},{9,1... | collective-permute-start | bytes 2457608 | tf_op jit(solution)/shard_map/ppermute | solution.py:295
  29.7 18.7 %collective-permute-start.5 = (bf16[128,3200]{1,0:T(8,128)(2,1)S(1)}, bf16[128,3200]{1,0:T(8,128)(2,1)S(1)}, u32[]{:S(2)}, u32[]{:S(2)}) collective-permute-start(bf16[128,3200]{1,0:T(8,128)(2,1)S(1)} %collective-permute-done.refs_8_), channel_id=1, source_target_pairs={{0,4},{2,6},{4,0},{6,2},{8,12},{10,14},{12,8},{14,10},{16,20},{18,... | collective-permute-start | bytes 2457608 | tf_op jit(solution)/shard_map/ppermute | solution.py:295
  31.3 17.7 %collective-permute-start.3 = (bf16[128,3200]{1,0:T(8,128)(2,1)}, bf16[128,3200]{1,0:T(8,128)(2,1)}, u32[]{:S(2)}, u32[]{:S(2)}) collective-permute-start(bf16[128,3200]{1,0:T(8,128)(2,1)} %collective-permute-done.1), channel_id=1, source_target_pairs={{8,0},{10,2},{12,4},{14,6},{16,24},{18,26},{20,28},{22,30},{9,1},{... | collective-permute-start | bytes 2457608 | tf_op jit(solution)/shard_map/ppermute | solution.py:295
  33.6 12.1 %collective-permute-start.6 = (bf16[2,128,1024]{2,1,0:T(8,128)(2,1)S(1)}, bf16[2,128,1024]{2,1,0:T(8,128)(2,1)S(1)}, u32[]{:S(2)}, u32[]{:S(2)}) collective-permute-start(bf16[2,128,1024]{2,1,0:T(8,128)(2,1)S(1)} %pad_maximum_fusion.1), channel_id=1, source_target_pairs={{0,1},{1,0},{2,3},{3,2},{4,5},{5,4},{6,7},{7,6},{8,9},{9,8},{10,11... | collective-permute-start | bytes 1572872 | tf_op jit(solution)/shard_map/ppermute | solution.py:306
  49.0 24.1 %collective-permute-start.7 = (bf16[128,3200]{1,0:T(8,128)(2,1)}, bf16[128,3200]{1,0:T(8,128)(2,1)}, u32[]{:S(2)}, u32[]{:S(2)}) collective-permute-start(bf16[128,3200]{1,0:T(8,128)(2,1)} %collective-permute-done.4), channel_id=1, source_target_pairs={{8,0},{10,2},{12,4},{14,6},{16,24},{18,26},{20,28},{22,30},{9,1},{... | collective-permute-start | bytes 2457608 | tf_op jit(solution)/shard_map/ppermute | solution.py:295
  55.6 17.6 %collective-permute-start.8 = (bf16[128,3200]{1,0:T(8,128)(2,1)S(1)}, bf16[128,3200]{1,0:T(8,128)(2,1)}, u32[]{:S(2)}, u32[]{:S(2)}) collective-permute-start(bf16[128,3200]{1,0:T(8,128)(2,1)S(1)} %broadcast_select_fusion.1.refs_0_), channel_id=1, source_target_pairs={{0,4},{2,6},{4,0},{6,2},{8,12},{10,14},{12,8},{14,10},{16,20},{18,... | collective-permute-start | bytes 2457608 | tf_op jit(solution)/shard_map/ppermute | solution.py:295
  58.6 16.4 %collective-permute-start.15 = (bf16[128,3200]{1,0:T(8,128)(2,1)S(1)}, bf16[128,3200]{1,0:T(8,128)(2,1)S(1)}, u32[]{:S(2)}, u32[]{:S(2)}) collective-permute-start(bf16[128,3200]{1,0:T(8,128)(2,1)S(1)} %concatenate.6.refs_0_), channel_id=1, source_target_pairs={{0,2},{2,0},{4,6},{6,4},{8,10},{10,8},{12,14},{14,12},{16,18},{18,... | collective-permute-start | bytes 2457608 | tf_op jit(solution)/shard_map/ppermute | solution.py:295
  58.6 17.5 %collective-permute-start.16 = (bf16[128,3200]{1,0:T(8,128)(2,1)}, bf16[128,3200]{1,0:T(8,128)(2,1)S(1)}, u32[]{:S(2)}, u32[]{:S(2)}) collective-permute-start(bf16[128,3200]{1,0:T(8,128)(2,1)} %copy-done.4), channel_id=1, source_target_pairs={{0,2},{2,0},{4,6},{6,4},{8,10},{10,8},{12,14},{14,12},{16,18},{18,... | collective-permute-start | bytes 2457608 | tf_op jit(solution)/shard_map/ppermute | solution.py:295
  76.0 23.2 %collective-permute-start.10 = (bf16[128,3200]{1,0:T(8,128)(2,1)S(1)}, bf16[128,3200]{1,0:T(8,128)(2,1)S(1)}, u32[]{:S(2)}, u32[]{:S(2)}) collective-permute-start(bf16[128,3200]{1,0:T(8,128)(2,1)S(1)} %broadcast_select_fusion.refs_8_), channel_id=1, source_target_pairs={{0,4},{2,6},{4,0},{6,2},{8,12},{10,14},{12,8},{14,10},{16,20},{18,... | collective-permute-start | bytes 2457608 | tf_op jit(solution)/shard_map/ppermute | solution.py:295
  76.6 22.6 %collective-permute-start.14 = (bf16[128,3200]{1,0:T(8,128)(2,1)S(1)}, bf16[128,3200]{1,0:T(8,128)(2,1)S(1)}, u32[]{:S(2)}, u32[]{:S(2)}) collective-permute-start(bf16[128,3200]{1,0:T(8,128)(2,1)S(1)} %broadcast_select_fusion.refs_8_), channel_id=1, source_target_pairs={{0,2},{2,0},{4,6},{6,4},{8,10},{10,8},{12,14},{14,12},{16,18},{18,... | collective-permute-start | bytes 2457608 | tf_op jit(solution)/shard_map/ppermute | solution.py:295
  76.8 22.4 %collective-permute-start.12 = (bf16[128,3200]{1,0:T(8,128)(2,1)S(1)}, bf16[128,3200]{1,0:T(8,128)(2,1)S(1)}, u32[]{:S(2)}, u32[]{:S(2)}) collective-permute-start(bf16[128,3200]{1,0:T(8,128)(2,1)S(1)} %broadcast_select_fusion.1.refs_0_), channel_id=1, source_target_pairs={{0,2},{2,0},{4,6},{6,4},{8,10},{10,8},{12,14},{14,12},{16,18},{18,... | collective-permute-start | bytes 2457608 | tf_op jit(solution)/shard_map/ppermute | solution.py:295
  77.1 22.1 %collective-permute-start.13 = (bf16[128,3200]{1,0:T(8,128)(2,1)}, bf16[128,3200]{1,0:T(8,128)(2,1)S(1)}, u32[]{:S(2)}, u32[]{:S(2)}) collective-permute-start(bf16[128,3200]{1,0:T(8,128)(2,1)} %collective-permute-done.8.refs_1_), channel_id=1, source_target_pairs={{0,2},{2,0},{4,6},{6,4},{8,10},{10,8},{12,14},{14,12},{16,18},{18,... | collective-permute-start | bytes 2457608 | tf_op jit(solution)/shard_map/ppermute | solution.py:295
  77.5 21.8 %collective-permute-start.11 = (bf16[3,128,1024]{2,1,0:T(8,128)(2,1)S(1)}, bf16[3,128,1024]{2,1,0:T(8,128)(2,1)S(1)}, u32[]{:S(2)}, u32[]{:S(2)}) collective-permute-start(bf16[3,128,1024]{2,1,0:T(8,128)(2,1)S(1)} %pad_maximum_fusion), channel_id=1, source_target_pairs={{0,1},{1,0},{2,3},{3,2},{4,5},{5,4},{6,7},{7,6},{8,9},{9,8},{10,11... | collective-permute-start | bytes 2359304 | tf_op jit(solution)/shard_map/ppermute | solution.py:306
  113.1 25.3 %collective-permute-start.25 = (bf16[4,128,1024]{2,1,0:T(8,128)(2,1)S(1)}, bf16[4,128,1024]{2,1,0:T(8,128)(2,1)S(1)}, u32[]{:S(2)}, u32[]{:S(2)}) collective-permute-start(bf16[4,128,1024]{2,1,0:T(8,128)(2,1)S(1)} %get-tuple-element.167), channel_id=1, source_target_pairs={{0,1},{1,0},{2,3},{3,2},{4,5},{5,4},{6,7},{7,6},{8,9},{9,8},{10,11... | collective-permute-start | bytes 3145736 | tf_op jit(solution)/shard_map/ppermute | solution.py:306
  113.7 24.9 %collective-permute-start.26 = (bf16[4,128,1024]{2,1,0:T(8,128)(2,1)S(1)}, bf16[4,128,1024]{2,1,0:T(8,128)(2,1)S(1)}, u32[]{:S(2)}, u32[]{:S(2)}) collective-permute-start(bf16[4,128,1024]{2,1,0:T(8,128)(2,1)S(1)} %get-tuple-element.166), channel_id=1, source_target_pairs={{0,4},{2,6},{4,0},{6,2},{8,12},{10,14},{12,8},{14,10},{16,20},{18,... | collective-permute-start | bytes 3145736 | tf_op jit(solution)/shard_map/ppermute | solution.py:295
  138.6 17.5 %collective-permute-start.28 = (bf16[16,128,1024]{2,1,0:T(8,128)(2,1)}, bf16[16,128,1024]{2,1,0:T(8,128)(2,1)S(1)}, u32[]{:S(2)}, u32[]{:S(2)}) collective-permute-start(bf16[16,128,1024]{2,1,0:T(8,128)(2,1)} %get-tuple-element.112), channel_id=1, source_target_pairs={{0,2},{2,0},{4,6},{6,4},{8,10},{10,8},{12,14},{14,12},{16,18},{18,... | collective-permute-start | bytes 12582920 | tf_op jit(solution)/shard_map/ppermute | solution.py:295
  141.0 13.9 %collective-permute-start.29 = (bf16[2,128,1024]{2,1,0:T(8,128)(2,1)S(1)}, bf16[2,128,1024]{2,1,0:T(8,128)(2,1)S(1)}, u32[]{:S(2)}, u32[]{:S(2)}) collective-permute-start(bf16[2,128,1024]{2,1,0:T(8,128)(2,1)S(1)} %get-tuple-element.165), channel_id=1, source_target_pairs={{0,4},{2,6},{4,0},{6,2},{8,12},{10,14},{12,8},{14,10},{16,20},{18,... | collective-permute-start | bytes 1572872 | tf_op jit(solution)/shard_map/ppermute | solution.py:295
  142.5 13.5 %collective-permute-start.30 = (bf16[2,128,1024]{2,1,0:T(8,128)(2,1)S(1)}, bf16[2,128,1024]{2,1,0:T(8,128)(2,1)S(1)}, u32[]{:S(2)}, u32[]{:S(2)}) collective-permute-start(bf16[2,128,1024]{2,1,0:T(8,128)(2,1)S(1)} %get-tuple-element.164), channel_id=1, source_target_pairs={{0,1},{1,0},{2,3},{3,2},{4,5},{5,4},{6,7},{7,6},{8,9},{9,8},{10,11... | collective-permute-start | bytes 1572872 | tf_op jit(solution)/shard_map/ppermute | solution.py:306
  159.2 15.2 %collective-permute-start.33 = (bf16[2,128,1024]{2,1,0:T(8,128)(2,1)}, bf16[2,128,1024]{2,1,0:T(8,128)(2,1)}, u32[]{:S(2)}, u32[]{:S(2)}) collective-permute-start(bf16[2,128,1024]{2,1,0:T(8,128)(2,1)} %get-tuple-element.161), channel_id=1, source_target_pairs={{0,1},{1,0},{2,3},{3,2},{4,5},{5,4},{6,7},{7,6},{8,9},{9,8},{10,11... | collective-permute-start | bytes 1572872 | tf_op jit(solution)/shard_map/ppermute | solution.py:306
  160.7 15.2 %collective-permute-start.34 = (bf16[2,128,1024]{2,1,0:T(8,128)(2,1)}, bf16[2,128,1024]{2,1,0:T(8,128)(2,1)}, u32[]{:S(2)}, u32[]{:S(2)}) collective-permute-start(bf16[2,128,1024]{2,1,0:T(8,128)(2,1)} %get-tuple-element.160), channel_id=1, source_target_pairs={{0,4},{2,6},{4,0},{6,2},{8,12},{10,14},{12,8},{14,10},{16,20},{18,... | collective-permute-start | bytes 1572872 | tf_op jit(solution)/shard_map/ppermute | solution.py:295
  165.8 19.8 %collective-permute-start.37 = (bf16[2,128,1024]{2,1,0:T(8,128)(2,1)S(1)}, bf16[2,128,1024]{2,1,0:T(8,128)(2,1)S(1)}, u32[]{:S(2)}, u32[]{:S(2)}) collective-permute-start(bf16[2,128,1024]{2,1,0:T(8,128)(2,1)S(1)} %pad_maximum_fusion.3), channel_id=1, source_target_pairs={{0,8},{2,10},{4,12},{6,14},{8,0},{10,2},{12,4},{14,6},{16,24},{18,... | collective-permute-start | bytes 1572872 | tf_op jit(solution)/shard_map/ppermute | solution.py:295
  165.9 19.8 %collective-permute-start.31 = (bf16[2,128,1024]{2,1,0:T(8,128)(2,1)}, bf16[2,128,1024]{2,1,0:T(8,128)(2,1)S(1)}, u32[]{:S(2)}, u32[]{:S(2)}) collective-permute-start(bf16[2,128,1024]{2,1,0:T(8,128)(2,1)} %get-tuple-element.163), channel_id=1, source_target_pairs={{0,1},{1,0},{2,3},{3,2},{4,5},{5,4},{6,7},{7,6},{8,9},{9,8},{10,11... | collective-permute-start | bytes 1572872 | tf_op jit(solution)/shard_map/ppermute | solution.py:306
  166.4 20.6 %collective-permute-start.32 = (bf16[2,128,1024]{2,1,0:T(8,128)(2,1)}, bf16[2,128,1024]{2,1,0:T(8,128)(2,1)S(1)}, u32[]{:S(2)}, u32[]{:S(2)}) collective-permute-start(bf16[2,128,1024]{2,1,0:T(8,128)(2,1)} %get-tuple-element.162), channel_id=1, source_target_pairs={{0,4},{2,6},{4,0},{6,2},{8,12},{10,14},{12,8},{14,10},{16,20},{18,... | collective-permute-start | bytes 1572872 | tf_op jit(solution)/shard_map/ppermute | solution.py:295
  177.5 12.8 %collective-permute-start.35 = (bf16[128,1024]{1,0:T(8,128)(2,1)S(1)}, bf16[128,1024]{1,0:T(8,128)(2,1)S(1)}, u32[]{:S(2)}, u32[]{:S(2)}) collective-permute-start(bf16[128,1024]{1,0:T(8,128)(2,1)S(1)} %get-tuple-element.159), channel_id=1, source_target_pairs={{0,4},{2,6},{4,0},{6,2},{8,12},{10,14},{12,8},{14,10},{16,20},{18,... | collective-permute-start | bytes 786440 | tf_op jit(solution)/shard_map/ppermute | solution.py:295
  178.1 12.2 %collective-permute-start.36 = (bf16[128,1024]{1,0:T(8,128)(2,1)S(1)}, bf16[128,1024]{1,0:T(8,128)(2,1)S(1)}, u32[]{:S(2)}, u32[]{:S(2)}) collective-permute-start(bf16[128,1024]{1,0:T(8,128)(2,1)S(1)} %get-tuple-element.158), channel_id=1, source_target_pairs={{0,1},{1,0},{2,3},{3,2},{4,5},{5,4},{6,7},{7,6},{8,9},{9,8},{10,11... | collective-permute-start | bytes 786440 | tf_op jit(solution)/shard_map/ppermute | solution.py:306
  192.1 13.7 %collective-permute-start.40 = (bf16[2,128,1024]{2,1,0:T(8,128)(2,1)S(1)}, bf16[2,128,1024]{2,1,0:T(8,128)(2,1)S(1)}, u32[]{:S(2)}, u32[]{:S(2)}) collective-permute-start(bf16[2,128,1024]{2,1,0:T(8,128)(2,1)S(1)} %pad_maximum_fusion.4), channel_id=1, source_target_pairs={{0,8},{2,10},{4,12},{6,14},{24,16},{26,18},{28,20},{30,22},{8,24},... | collective-permute-start | bytes 1572872 | tf_op jit(solution)/shard_map/ppermute | solution.py:295
  193.8 12.0 %collective-permute-start.38 = (bf16[128,1024]{1,0:T(8,128)(2,1)S(1)}, bf16[128,1024]{1,0:T(8,128)(2,1)S(1)}, u32[]{:S(2)}, u32[]{:S(2)}) collective-permute-start(bf16[128,1024]{1,0:T(8,128)(2,1)S(1)} %get-tuple-element.155), channel_id=1, source_target_pairs={{0,4},{2,6},{4,0},{6,2},{8,12},{10,14},{12,8},{14,10},{16,20},{18,... | collective-permute-start | bytes 786440 | tf_op jit(solution)/shard_map/ppermute | solution.py:295
  207.6 27.1 %collective-permute-start.42 = (bf16[2,128,1024]{2,1,0:T(8,128)(2,1)S(1)}, bf16[2,128,1024]{2,1,0:T(8,128)(2,1)S(1)}, u32[]{:S(2)}, u32[]{:S(2)}) collective-permute-start(bf16[2,128,1024]{2,1,0:T(8,128)(2,1)S(1)} %fusion), channel_id=1, source_target_pairs={{8,16},{10,18},{12,20},{14,22},{16,8},{18,10},{20,12},{22,14},{9,1... | collective-permute-start | bytes 1572872 | tf_op jit(solution)/shard_map/ppermute | solution.py:295
  210.1 24.6 %collective-permute-start.41 = (bf16[2,128,1024]{2,1,0:T(8,128)(2,1)S(1)}, bf16[2,128,1024]{2,1,0:T(8,128)(2,1)S(1)}, u32[]{:S(2)}, u32[]{:S(2)}) collective-permute-start(bf16[2,128,1024]{2,1,0:T(8,128)(2,1)S(1)} %pad_maximum_fusion.5), channel_id=1, source_target_pairs={{0,24},{2,26},{4,28},{6,30},{24,0},{26,2},{28,4},{30,6},{1,25},{3,... | collective-permute-start | bytes 1572872 | tf_op jit(solution)/shard_map/ppermute | solution.py:295
  (31 other events, 375.9 us)

commit v2 on v1

--- a/solution.py
+++ b/solution.py
@@ -21,14 +21,20 @@
     into.append(copy)
 
 
-def rounds_kernel(cap, count, index, at_ref, *refs):
+def rounds_kernel(cap, count, index, split, at_ref, *refs):
     views = [ref if i is None else ref.at[i] for ref, i in zip(refs, index)]
     groups = [views[8 * i:8 * i + 8] for i in range(count)]
     blocks = [group[b] for group in groups for b in range(4)]
     others = [group[4 + b] for group in groups for b in range(4)]
-    (wg, wu, wd, xs, cs, hs, keep, send, gp,
-     x, c, tab, wgu, wdv, xp, cp, hp, row,
-     sem_x, sem_c, sem_t, sem_w, sem_o) = refs[8 * count:]
+    wg, wu, wd, xs, cs, hs, gp = refs[8 * count:8 * count + 7]
+    split_n = count if split else 1
+    results = [refs[8 * count + 7 + k * split_n:8 * count + 7 + (k + 1) * split_n] for k in range(2)]
+    (x, c, tab, wgu, wdv, xp, cp, hp, row,
+     sem_x, sem_c, sem_t, sem_w, sem_o) = refs[8 * count + 7 + 2 * split_n:]
+
+    def slot(i, layer):
+        return layer * 8 + i if split else i * count + layer
+
     rows = blocks[0].shape[0]
     pairs = 2 * count
     local, width, hid = wg.shape
@@ -130,10 +136,12 @@
         for y, at in enumerate((mine, theirs)):
             part = dot(picks[k], row[k, :, pl.ds(at, half)], (1, 0)).astype(BF)
             for b in range(2):
-                (outk, outs)[k % 2][(y * 2 + b) * count + k // 2] = part[b * rows:(b + 1) * rows]
+                (outk, outs)[k % 2][slot(y * 2 + b, k // 2)] = part[b * rows:(b + 1) * rows]
     for k in range(2):
-        half_out = pl.ds(0, 4 * count)
-        begin((outk, outs)[k].at[half_out], (keep, send)[k].at[half_out], sem_o.at[3 + k], o_copies)
+        for r in range(split_n):
+            size = 4 * count // split_n
+            begin((outk, outs)[k].at[pl.ds(r * 8, size)], results[k][r].at[pl.ds(0, size)],
+                  sem_o.at[3 + 2 * k + r], o_copies)
     for e in range(local):
         out = dot(hp[e, :, hid:], wgu[e], (1, 1)).astype(BF)
         for k in range(pairs):
@@ -142,10 +150,11 @@
         for y, at in enumerate((mine, theirs)):
             part = dot(picks[k], row[k, :, pl.ds(at, half)], (1, 0)).astype(BF)
             for b in range(2):
-                (outk, outs)[k % 2][(4 + b * 2 + y) * count + k // 2] = part[b * rows:(b + 1) * rows]
+                (outk, outs)[k % 2][slot(4 + b * 2 + y, k // 2)] = part[b * rows:(b + 1) * rows]
         for b in range(4):
-            slot = (4 + b) * count + k // 2
-            begin((outk, outs)[k % 2].at[slot], (keep, send)[k % 2].at[slot], sem_o.at[5 + 4 * k + b], o_copies)
+            held_at = slot(4 + b, k // 2)
+            into = results[k % 2][k // 2].at[4 + b] if split else results[k % 2][0].at[held_at]
+            begin((outk, outs)[k % 2].at[held_at], into, sem_o.at[7 + 4 * k + b], o_copies)
     for k in range(pairs):
         prod = jnp.concatenate([v[k * chunk:(k + 1) * chunk] for v in prods], axis=0)
         high = prod.astype(BF).astype(F32)
@@ -157,7 +166,7 @@
         copy.wait()
 
 
-def rounds(at, pieces, cap, wg, wu, wd):
+def rounds(at, pieces, cap, wg, wu, wd, split):
     count = len(pieces) // 8
     pieces, index = zip(*(p if isinstance(p, tuple) else (p, None) for p in pieces))
     rows = pieces[0].shape[0]
@@ -166,19 +175,20 @@
     n = count * 4 * rows
     wide = pieces[0].shape[1] - width - half
     packed = count * 4 * cap
+    each = 8 if split else 8 * count
+    results = [jax.ShapeDtypeStruct((each, rows, half), BF)] * (16 * count // each)
     anyspec = pl.BlockSpec(memory_space=pl.ANY)
     vspec = pl.BlockSpec(memory_space=pltpu.VMEM)
     return pl.pallas_call(
-        functools.partial(rounds_kernel, cap, count, index),
+        functools.partial(rounds_kernel, cap, count, index, split),
         in_specs=[pl.BlockSpec(memory_space=pltpu.SMEM)] + [anyspec] * (8 * count + 3),
-        out_specs=[anyspec] * 5 + [vspec],
+        out_specs=[anyspec] * 3 + [vspec] + [anyspec] * len(results),
         out_shape=[
             jax.ShapeDtypeStruct((local, packed, width), BF),
             jax.ShapeDtypeStruct((local, packed, width), BF),
             jax.ShapeDtypeStruct((local, packed, 3 * hid), BF),
-            jax.ShapeDtypeStruct((8 * count, rows, half), BF),
-            jax.ShapeDtypeStruct((8 * count, rows, half), BF),
             jax.ShapeDtypeStruct((8, n), F32),
+            *results,
         ],
         scratch_shapes=[
             pltpu.VMEM((8 * count, rows, half), BF),
@@ -194,7 +204,7 @@
             pltpu.SemaphoreType.DMA((8 * count,)),
             pltpu.SemaphoreType.DMA((4 * count,)),
             pltpu.SemaphoreType.DMA((3 * local,)),
-            pltpu.SemaphoreType.DMA((5 + 8 * count,)),
+            pltpu.SemaphoreType.DMA((7 + 8 * count,)),
         ],
         compiler_params=pltpu.CompilerParams(vmem_limit_bytes=44 * 1024 * 1024),
         cost_estimate=pl.CostEstimate(
@@ -317,8 +327,8 @@
     cap = 3 * rows * routes.shape[1] // (2 * experts)
     at = jnp.stack([col, place * local]).astype(jnp.int32)
 
-    def run(*pieces):
-        return rounds(at, pieces, cap, w_gate, w_up, w_down)
+    def run(*pieces, split=False):
+        return rounds(at, pieces, cap, w_gate, w_up, w_down, split)
 
     def stage_one(keep, got):
         return over_y(add16(keep[4:8], got[4:8])), over_x(add16(keep[12:16], got[12:16]))
@@ -348,7 +358,7 @@
     x3, y2 = over_x(l3), over_y(cotangents(l2, x2, l3))
     ky1 = over_core(y1)
     k2, kx2, k3 = over_core(l2), over_core(x2), over_core(l3)
-    xs_a, cs_a, hs_a, keep_a, send_a, gp_a = run(
+    xs_a, cs_a, hs_a, gp_a, keep_a, send_a = run(
         l0, x0, k0, kx0, (y0, 0), (y0, 1), (ky0, 0), (ky0, 1),
         l1, x1, k1, kx1, (y1, 0), (y1, 1), (ky1, 0), (ky1, 1))
     l2, x2, l3, x3, y2, k2, kx2, k3, keep_a, send_a = sync(
@@ -360,43 +370,41 @@
 
     kyx3 = over_core(yx3)
     one_a = stage_one(keep_a, got_a)
-    xs_b, cs_b, hs_b, keep_b, send_b, gp_b = run(
+    xs_b, cs_b, hs_b, gp_b, keep2, keep3, send2, send3 = run(
         l2, x2, k2, kx2, (y2, 0), (y2, 1), (ky2, 0), (ky2, 1),
-        l3, x3, k3, kx3, (y2, 2), (yx3, 0), (ky2, 2), (kyx3, 0))
-    one_a, keep_b, send_b = sync((one_a, keep_b, send_b))
-
-    got_b = over_core(send_b)
+        l3, x3, k3, kx3, (y2, 2), (yx3, 0), (ky2, 2), (kyx3, 0), split=True)
+    one_a, keep2, keep3, send2, send3 = sync((one_a, keep2, keep3, send2, send3))
+
+    got2, got3 = over_core(send2), over_core(send3)
     two_a = stage_two(keep_a, got_a, *one_a)
-    got_b, two_a = sync((got_b, two_a))
-
-    def first_sums(i):
-        return over_y(add16(keep_b[4 + i:8:2], got_b[4 + i:8:2])), over_x(add16(keep_b[12 + i:16:2], got_b[12 + i:16:2]))
-
-    def second_sums(i, one):
-        return (over_x(add16(keep_b[2 + i], got_b[2 + i], one[0][1])),
-                over_y(add16(keep_b[10 + i], got_b[10 + i], one[1][1])))
-
-    def whole_sum(i, one, two):
-        return jnp.stack([add16(keep_b[i], got_b[i], one[0][0], two[0]),
-                          add16(keep_b[8 + i], got_b[8 + i], one[1][0], two[1])])
-
-    one_2 = first_sums(0)
+    got2, keep2 = sync((got2, keep2))
+
+    def first_sums(keep, got):
+        return over_y(add16(keep[2:4], got[2:4])), over_x(add16(keep[6:8], got[6:8]))
+
+    def second_sums(keep, got, one):
+        return over_x(add16(keep[1], got[1], one[0][1])), over_y(add16(keep[5], got[5], one[1][1]))
+
+    def whole_sum(keep, got, one, two):
+        return jnp.stack([add16(keep[0], got[0], one[0][0], two[0]), add16(keep[4], got[4], one[1][0], two[1])])
+
+    one_2 = first_sums(keep2, got2)
     gps = jnp.concatenate([gp_a[:local], gp_b[:local]], axis=1).reshape(local, 4, 4, rows)
     gps = gps[:, :, jnp.array([0, 2, 1, 3])].reshape(local, owners, rows).transpose(1, 0, 2)
     gps = gps[jnp.arange(owners) ^ place]
-    one_2, gps = sync((one_2, gps))
-
-    one_3, two_2 = first_sums(1), second_sums(0, one_2)
+    one_2, two_a, gps = sync((one_2, two_a, gps))
+
+    one_3, two_2 = first_sums(keep3, got3), second_sums(keep2, got2, one_2)
     from1 = over_z(layer_sum(keep_a, got_a, one_a, two_a, 1).astype(BF))
     grad_gate, grad_up = weight_grads([xs_a, xs_b], [hs_a, hs_b], hid, 2 * hid, 2, w_gate.shape, "grad_in")
     one_3, two_2, from1, grad_gate, grad_up = sync((one_3, two_2, from1, grad_gate, grad_up))
 
-    two_3 = second_sums(1, one_3)
-    step = leap(whole_sum(0, one_2, two_2))
+    two_3 = second_sums(keep3, got3, one_3)
+    step = leap(whole_sum(keep2, got2, one_2, two_2))
     back = lax.all_to_all(gps, "dp", 0, 0, tiled=True)
     two_3, step, back = sync((two_3, step, back))
 
-    sum3 = whole_sum(1, one_3, two_3)
+    sum3 = whole_sum(keep3, got3, one_3, two_3)
     ends, inner = end_to_end(sum3), across(add16(sum3, step))
     other_back = over_y(back)
     (grad_down,) = weight_grads([cs_a, cs_b], [hs_a, hs_b], 0, hid, 1, w_down.shape, "grad_down")

time: 240 us -> 236 us (0.983)
  waiting for transfers between devices: 101 us -> 93.7 us
  starting transfers between devices: 43.3 us -> 46.6 us
    ppermute x33 -> x34, waiting for transfers between devices: 63.2 us -> 51.5 us  [permute(): return lambda v: lax.ppermute(v, 'dp', pairs)]
    ppermute x11, waiting for transfers between devices: 37.4 us -> 42.2 us  [over_y(): return lax.ppermute(v, 'col', [(0, 1), (1, 0)])]
    ppermute x33 -> x34, starting transfers between devices: 31.5 us -> 34.5 us  [permute(): return lambda v: lax.ppermute(v, 'dp', pairs)]
    convert_element_type x7 -> x8, other arithmetic: 12.4 us -> 13.8 us  [add16(): return add(*terms).astype(BF)]
  transfers between devices with their start and end apart: 44 -> 45, of which waited for: 21 -> 20; matrix products, arithmetic and copies ran while one was open for 6% -> 8% of each run, Pallas kernels for 22% -> 22%
where the time goes in v2:
time: 236 us; the launch traced here: 233 us
  waiting for transfers between devices  93.7 us (40%)
  Pallas kernels  51.2 us (22%)
  starting transfers between devices  46.6 us (20%)
  other arithmetic  24.9 us (11%)
  blocking collectives  10.2 us (4%)
  local copies, waits for them, and re-layouts  4.8 us (2%)
    ppermute x34, waiting for transfers between devices, permute(): return lambda v: lax.ppermute(v, 'dp', pairs)  51.5 us
    ppermute x11, waiting for transfers between devices, over_y(): return lax.ppermute(v, 'col', [(0, 1), (1, 0)])  42.2 us
    pallas_call x2, Pallas kernels, rounds(): pl.pallas_call(functools.partial(rounds_kernel, cap, count, index, split)...  39.8 us
    ppermute x34, starting transfers between devices, permute(): return lambda v: lax.ppermute(v, 'dp', pairs)  34.5 us
    convert_element_type x8, other arithmetic, add16(): return add(*terms).astype(BF)  13.8 us
    ppermute x11, starting transfers between devices, over_y(): return lax.ppermute(v, 'col', [(0, 1), (1, 0)])  12.1 us
    pallas_call x2, Pallas kernels, weight_grads(): pl.pallas_call(functools.partial(weight_kernel, rounds, off, outs_n), in_...  11.4 us
    all_to_all x1, blocking collectives, body16(): back = lax.all_to_all(gps, 'dp', 0, 0, tiled=True)  10.2 us
  transfers between devices with their start and end apart: 45, of which 20 were waited for; matrix products, arithmetic and copies ran while one was open for 8% of the time, Pallas kernels for 22%

profile of v2, /device:TPU:8, one launch (start us, length us, event | category | flops | bytes accessed | tf_op | source)
XLA Modules:
  0.0 232.9 jit_solution(4405285991474146950)
XLA Ops:
  3.0 5.0 %collective-permute-start.1 = (bf16[128,3200]{1,0:T(8,128)(2,1)S(1)}, bf16[128,3200]{1,0:T(8,128)(2,1)}, u32[]{:S(2)}, u32[]{:S(2)}) collective-permute-start(bf16[128,3200]{1,0:T(8,128)(2,1)S(1)} %concatenate.6.refs_0_), channel_id=1, source_target_pairs={{8,16},{10,18},{12,20},{14,22},{16,8},{18,10},{20,12},{22,14},{9,1... | collective-permute-start | bytes 2457608 | tf_op jit(solution)/shard_map/ppermute | solution.py:305
  8.0 1.6 collective-permute-start.2
  9.6 13.4 %collective-permute-done.refs_8_ = bf16[128,3200]{1,0:T(8,128)(2,1)S(1)} collective-permute-done((bf16[128,3200]{1,0:T(8,128)(2,1)S(1)}, bf16[128,3200]{1,0:T(8,128)(2,1)S(1)}, u32[]{:S(2)}, u32[]{:S(2)}) %collective-permute-start) | collective-permute-done | bytes 819232 | tf_op jit(solution)/shard_map/ppermute | solution.py:305
  22.9 3.1 %collective-permute-done.1 = bf16[128,3200]{1,0:T(8,128)(2,1)} collective-permute-done((bf16[128,3200]{1,0:T(8,128)(2,1)S(1)}, bf16[128,3200]{1,0:T(8,128)(2,1)}, u32[]{:S(2)}, u32[]{:S(2)}) %collective-permute-start.1) | collective-permute-done | bytes 819232 | tf_op jit(solution)/shard_map/ppermute | solution.py:305
  27.5 2.2 collective-permute-start.4
  29.7 1.6 collective-permute-start.5
  31.3 2.2 collective-permute-start.3
  33.6 1.6 collective-permute-start.6
  35.2 10.5 %collective-permute-done.6.refs_4_.refs_5_ = bf16[2,128,1024]{2,1,0:T(8,128)(2,1)S(1)} collective-permute-done((bf16[2,128,1024]{2,1,0:T(8,128)(2,1)S(1)}, bf16[2,128,1024]{2,1,0:T(8,128)(2,1)S(1)}, u32[]{:S(2)}, u32[]{:S(2)}) %collective-permute-start.6) | collective-permute-done | bytes 524320 | tf_op jit(solution)/shard_map/ppermute | solution.py:316
  45.7 2.4 %collective-permute-done.4 = bf16[128,3200]{1,0:T(8,128)(2,1)} collective-permute-done((bf16[128,3200]{1,0:T(8,128)(2,1)S(1)}, bf16[128,3200]{1,0:T(8,128)(2,1)}, u32[]{:S(2)}, u32[]{:S(2)}) %collective-permute-start.4) | collective-permute-done | bytes 819232 | tf_op jit(solution)/shard_map/ppermute | solution.py:305
  49.0 5.3 %collective-permute-start.7 = (bf16[128,3200]{1,0:T(8,128)(2,1)}, bf16[128,3200]{1,0:T(8,128)(2,1)}, u32[]{:S(2)}, u32[]{:S(2)}) collective-permute-start(bf16[128,3200]{1,0:T(8,128)(2,1)} %collective-permute-done.4), channel_id=1, source_target_pairs={{8,0},{10,2},{12,4},{14,6},{16,24},{18,26},{20,28},{22,30},{9,1},{... | collective-permute-start | bytes 2457608 | tf_op jit(solution)/shard_map/ppermute | solution.py:305
  59.0 9.1 %collective-permute-done.9.refs_12_.refs_13_ = bf16[2,128,1024]{2,1,0:T(8,128)(2,1)} collective-permute-done((bf16[2,128,1024]{2,1,0:T(8,128)(2,1)}, bf16[2,128,1024]{2,1,0:T(8,128)(2,1)}, u32[]{:S(2)}, u32[]{:S(2)}) %collective-permute-start.9) | collective-permute-done | bytes 524320 | tf_op jit(solution)/shard_map/ppermute | solution.py:316
  68.1 5.0 %collective-permute-done.8.refs_1_ = bf16[128,3200]{1,0:T(8,128)(2,1)} collective-permute-done((bf16[128,3200]{1,0:T(8,128)(2,1)S(1)}, bf16[128,3200]{1,0:T(8,128)(2,1)}, u32[]{:S(2)}, u32[]{:S(2)}) %collective-permute-start.8) | collective-permute-done | bytes 819232 | tf_op jit(solution)/shard_map/ppermute | solution.py:305
  77.5 1.6 collective-permute-start.11
  79.2 20.1 %moe_rounds.2 = (bf16[2,384,2048]{2,1,0:T(8,128)(2,1)}, bf16[2,384,2048]{2,1,0:T(8,128)(2,1)}, bf16[2,384,1152]{2,1,0:T(8,128)(2,1)}, f32[8,1024]{1,0:T(8,128)S(...) custom-call(s32[2]{0:T(128)S(1)} %pad_add_fusion.at_ref, bf16[128,3200]{1,0:T(8,128)(2,1)S(1)} %concatenate.6.refs_0_, ...), custom_call_target="tpu_custom_call" | custom-call | flops 7247757312 | bytes 34603008 | tf_op jit(solution)/shard_map/moe_rounds/pallas_call | solution.py:182
  100.6 8.1 %collective-permute-done.21.refs_13_ = bf16[1,128,1024]{2,1,0:T(8,128)(2,1)S(1)} collective-permute-done((bf16[1,128,1024]{2,1,0:T(8,128)(2,1)S(1)}, bf16[1,128,1024]{2,1,0:T(8,128)(2,1)S(1)}, u32[]{:S(2)}, u32[]{:S(2)}) %collective-permute-start.21) | collective-permute-done | bytes 262176 | tf_op jit(solution)/shard_map/ppermute | solution.py:316
  109.1 4.0 %add_convert_fusion = (bf16[4,128,1024]{2,1,0:T(8,128)(2,1)S(1)}, bf16[4,128,1024]{2,1,0:T(8,128)(2,1)S(1)}) fusion(bf16[16,128,1024]{2,1,0:T(8,128)(2,1)S(1)} %collective-permute-done.24, bf16[16,128,1024]{2,1,0:T(8,128)(2,1)} %get-tuple-element.103), kind=kLoop, calls=%fused_computation.2 | loop fusion | flops 4194304 | bytes 6291456 | tf_op jit(solution)/shard_map/convert_element_type | solution.py:290
  116.7 19.7 %moe_rounds.3 = (bf16[2,384,2048]{2,1,0:T(8,128)(2,1)}, bf16[2,384,2048]{2,1,0:T(8,128)(2,1)}, bf16[2,384,1152]{2,1,0:T(8,128)(2,1)}, f32[8,1024]{1,0:T(8,128)S(...) custom-call(s32[2]{0:T(128)S(1)} %pad_add_fusion.at_ref, ...), custom_call_target="tpu_custom_call" | custom-call | flops 7247757312 | bytes 34603008 | tf_op jit(solution)/shard_map/moe_rounds/pallas_call | solution.py:182
  136.4 2.0 collective-permute-done.25
  139.2 3.0 %add_convert_fusion.4 = (bf16[2,128,1024]{2,1,0:T(8,128)(2,1)}, bf16[2,128,1024]{2,1,0:T(8,128)(2,1)}) fusion(bf16[4,128,1024]{2,1,0:T(8,128)(2,1)S(1)} %collective-permute-done.26, bf16[16,128,1024]{2,1,0:T(8,128)(2,1)S(1)} %collective-permute-done.24, bf16[16,128,1024]{2,1,0:T(8,128)(2,1)} %get-tuple-element.103, ...), kind=kLoop, calls=%fused_computation.13 | loop fusion | flops 3145728 | bytes 4194304 | tf_op jit(solution)/shard_map/convert_element_type | solution.py:290
  142.2 1.6 collective-permute-start.31
  151.7 1.8 add_convert_fusion.2
  154.0 3.3 %collective-permute-done.31 = bf16[2,128,1024]{2,1,0:T(8,128)(2,1)} collective-permute-done((bf16[2,128,1024]{2,1,0:T(8,128)(2,1)}, bf16[2,128,1024]{2,1,0:T(8,128)(2,1)}, u32[]{:S(2)}, u32[]{:S(2)}) %collective-permute-start.31) | collective-permute-done | bytes 524320 | tf_op jit(solution)/shard_map/ppermute | solution.py:305
  158.9 11.2 %collective-permute-done.29 = bf16[2,128,1024]{2,1,0:T(8,128)(2,1)} collective-permute-done((bf16[2,128,1024]{2,1,0:T(8,128)(2,1)}, bf16[2,128,1024]{2,1,0:T(8,128)(2,1)}, u32[]{:S(2)}, u32[]{:S(2)}) %collective-permute-start.29) | collective-permute-done | bytes 524320 | tf_op jit(solution)/shard_map/ppermute | solution.py:316
  170.1 3.0 %add_convert_fusion.11 = (bf16[1,128,1024]{2,1,0:T(8,128)(2,1)S(1)}, f32[1,128,1024]{2,1,0:T(8,128)S(1)}, f32[1,128,1024]{2,1,0:T(8,128)S(1)}, bf16[1,128,1024]{2,1,0:T(8,128)(2,1)S(1)}) fusion(bf16[2,128,1024]{2,1,0:T(8,128)(2,1)} %collective-permute-done.31, bf16[4,128,1024]{2,1,0:T(8,128)(2,1)S(1)} %copy-done.16, bf16[16,128,1024]{2,1,0:T(8,128)(2,1)} %copy-done.10, ...), kind=kLoop, calls=%fused_computation.37 | loop fusion | flops 3932160 | bytes 5767168 | tf_op jit(solution)/shard_map/convert
  173.3 1.6 fusion.10
  177.0 7.0 %grad_in.1 = (bf16[2,2048,384]{2,1,0:T(8,128)(2,1)}, bf16[2,2048,384]{2,1,0:T(8,128)(2,1)}) custom-call(bf16[2,384,2048]{2,1,0:T(8,128)(2,1)S(1)} %copy-done.9, bf16[2,384,2048]{2,1,0:T(8,128)(2,1)S(1)} %copy-done.8, bf16[2,384,1152]{2,1,0:T(8,128)(2,1)S(1)} %copy-done.2, bf16[2,384,1152]{2,1,0:T(8,128)(2,1)S(1)} %copy-done.3), custom_call_target="tpu_custom_call" | custom-call | flops 4831838208 | bytes 14942208 | tf_op jit(solution)/shard_map/grad_in/pallas_call | solution.py:256
  189.6 1.6 collective-permute-start.39
  191.7 10.2 %all_to_all.5 = f32[16,2,128]{2,1,0:T(2,128)S(1)} all-to-all(f32[16,2,128]{2,1,0:T(2,128)S(1)} %gather_fusion.1), channel_id=1, replica_groups=mesh['dp'=16,'col'=2] {'dp'}, dimensions={0} | all-to-all | bytes 32768 | tf_op jit(solution)/shard_map/all_to_all | solution.py:404
  203.7 2.5 %collective-permute-start.43 = (bf16[2,128,1024]{2,1,0:T(8,128)(2,1)S(1)}, bf16[2,128,1024]{2,1,0:T(8,128)(2,1)S(1)}, u32[]{:S(2)}, u32[]{:S(2)}) collective-permute-start(bf16[2,128,1024]{2,1,0:T(8,128)(2,1)S(1)} %fusion), channel_id=1, source_target_pairs={{8,16},{10,18},{12,20},{14,22},{16,8},{18,10},{20,12},{22,14},{9,1... | collective-permute-start | bytes 1572872 | tf_op jit(solution)/shard_map/ppermute | solution.py:305
  207.6 4.5 %grad_down.1 = bf16[2,384,2048]{2,1,0:T(8,128)(2,1)} custom-call(bf16[2,384,2048]{2,1,0:T(8,128)(2,1)S(1)} %copy-done, bf16[2,384,2048]{2,1,0:T(8,128)(2,1)S(1)} %copy-done.1, bf16[2,384,1152]{2,1,0:T(8,128)(2,1)S(1)} %copy-done.2, bf16[2,384,1152]{2,1,0:T(8,128)(2,1)S(1)} %copy-done.3), custom_call_target="tpu_custom_call" | custom-call | flops 2415919104 | bytes 10616832 | tf_op jit(solution)/shard_map/grad_down/pallas_call | solution.py:256
  212.1 18.7 %collective-permute-done.43 = bf16[2,128,1024]{2,1,0:T(8,128)(2,1)S(1)} collective-permute-done((bf16[2,128,1024]{2,1,0:T(8,128)(2,1)S(1)}, bf16[2,128,1024]{2,1,0:T(8,128)(2,1)S(1)}, u32[]{:S(2)}, u32[]{:S(2)}) %collective-permute-start.43) | collective-permute-done | bytes 524320 | tf_op jit(solution)/shard_map/ppermute | solution.py:305
  (152 shorter events, 43.2 us)
Async XLA Ops:
  2.9 20.0 %collective-permute-start = (bf16[128,3200]{1,0:T(8,128)(2,1)S(1)}, bf16[128,3200]{1,0:T(8,128)(2,1)S(1)}, u32[]{:S(2)}, u32[]{:S(2)}) collective-permute-start(bf16[128,3200]{1,0:T(8,128)(2,1)S(1)} %concatenate.6.refs_0_), channel_id=1, source_target_pairs={{0,8},{2,10},{4,12},{6,14},{8,0},{10,2},{12,4},{14,6},{16,24},{18,... | collective-permute-start | bytes 2457608 | tf_op jit(solution)/shard_map/ppermute | solution.py:305
  3.0 23.1 %collective-permute-start.1 = (bf16[128,3200]{1,0:T(8,128)(2,1)S(1)}, bf16[128,3200]{1,0:T(8,128)(2,1)}, u32[]{:S(2)}, u32[]{:S(2)}) collective-permute-start(bf16[128,3200]{1,0:T(8,128)(2,1)S(1)} %concatenate.6.refs_0_), channel_id=1, source_target_pairs={{8,16},{10,18},{12,20},{14,22},{16,8},{18,10},{20,12},{22,14},{9,1... | collective-permute-start | bytes 2457608 | tf_op jit(solution)/shard_map/ppermute | solution.py:305
  8.0 19.5 %collective-permute-start.2 = (bf16[128,3200]{1,0:T(8,128)(2,1)S(1)}, bf16[128,3200]{1,0:T(8,128)(2,1)S(1)}, u32[]{:S(2)}, u32[]{:S(2)}) collective-permute-start(bf16[128,3200]{1,0:T(8,128)(2,1)S(1)} %concatenate.6.refs_0_), channel_id=1, source_target_pairs={{0,4},{2,6},{4,0},{6,2},{8,12},{10,14},{12,8},{14,10},{16,20},{18,... | collective-permute-start | bytes 2457608 | tf_op jit(solution)/shard_map/ppermute | solution.py:305
  27.5 20.6 %collective-permute-start.4 = (bf16[128,3200]{1,0:T(8,128)(2,1)S(1)}, bf16[128,3200]{1,0:T(8,128)(2,1)}, u32[]{:S(2)}, u32[]{:S(2)}) collective-permute-start(bf16[128,3200]{1,0:T(8,128)(2,1)S(1)} %collective-permute-done.refs_8_), channel_id=1, source_target_pairs={{8,16},{10,18},{12,20},{14,22},{16,8},{18,10},{20,12},{22,14},{9,1... | collective-permute-start | bytes 2457608 | tf_op jit(solution)/shard_map/ppermute | solution.py:305
  29.7 18.7 %collective-permute-start.5 = (bf16[128,3200]{1,0:T(8,128)(2,1)S(1)}, bf16[128,3200]{1,0:T(8,128)(2,1)S(1)}, u32[]{:S(2)}, u32[]{:S(2)}) collective-permute-start(bf16[128,3200]{1,0:T(8,128)(2,1)S(1)} %collective-permute-done.refs_8_), channel_id=1, source_target_pairs={{0,4},{2,6},{4,0},{6,2},{8,12},{10,14},{12,8},{14,10},{16,20},{18,... | collective-permute-start | bytes 2457608 | tf_op jit(solution)/shard_map/ppermute | solution.py:305
  31.3 17.7 %collective-permute-start.3 = (bf16[128,3200]{1,0:T(8,128)(2,1)}, bf16[128,3200]{1,0:T(8,128)(2,1)}, u32[]{:S(2)}, u32[]{:S(2)}) collective-permute-start(bf16[128,3200]{1,0:T(8,128)(2,1)} %collective-permute-done.1), channel_id=1, source_target_pairs={{8,0},{10,2},{12,4},{14,6},{16,24},{18,26},{20,28},{22,30},{9,1},{... | collective-permute-start | bytes 2457608 | tf_op jit(solution)/shard_map/ppermute | solution.py:305
  33.6 12.1 %collective-permute-start.6 = (bf16[2,128,1024]{2,1,0:T(8,128)(2,1)S(1)}, bf16[2,128,1024]{2,1,0:T(8,128)(2,1)S(1)}, u32[]{:S(2)}, u32[]{:S(2)}) collective-permute-start(bf16[2,128,1024]{2,1,0:T(8,128)(2,1)S(1)} %pad_maximum_fusion.1), channel_id=1, source_target_pairs={{0,1},{1,0},{2,3},{3,2},{4,5},{5,4},{6,7},{7,6},{8,9},{9,8},{10,11... | collective-permute-start | bytes 1572872 | tf_op jit(solution)/shard_map/ppermute | solution.py:316
  49.0 24.1 %collective-permute-start.7 = (bf16[128,3200]{1,0:T(8,128)(2,1)}, bf16[128,3200]{1,0:T(8,128)(2,1)}, u32[]{:S(2)}, u32[]{:S(2)}) collective-permute-start(bf16[128,3200]{1,0:T(8,128)(2,1)} %collective-permute-done.4), channel_id=1, source_target_pairs={{8,0},{10,2},{12,4},{14,6},{16,24},{18,26},{20,28},{22,30},{9,1},{... | collective-permute-start | bytes 2457608 | tf_op jit(solution)/shard_map/ppermute | solution.py:305
  55.5 17.6 %collective-permute-start.8 = (bf16[128,3200]{1,0:T(8,128)(2,1)S(1)}, bf16[128,3200]{1,0:T(8,128)(2,1)}, u32[]{:S(2)}, u32[]{:S(2)}) collective-permute-start(bf16[128,3200]{1,0:T(8,128)(2,1)S(1)} %broadcast_select_fusion.1.refs_0_), channel_id=1, source_target_pairs={{0,4},{2,6},{4,0},{6,2},{8,12},{10,14},{12,8},{14,10},{16,20},{18,... | collective-permute-start | bytes 2457608 | tf_op jit(solution)/shard_map/ppermute | solution.py:305
  57.0 11.1 %collective-permute-start.9 = (bf16[2,128,1024]{2,1,0:T(8,128)(2,1)}, bf16[2,128,1024]{2,1,0:T(8,128)(2,1)}, u32[]{:S(2)}, u32[]{:S(2)}) collective-permute-start(bf16[2,128,1024]{2,1,0:T(8,128)(2,1)} %pad_maximum_fusion.2), channel_id=1, source_target_pairs={{0,1},{1,0},{2,3},{3,2},{4,5},{5,4},{6,7},{7,6},{8,9},{9,8},{10,11... | collective-permute-start | bytes 1572872 | tf_op jit(solution)/shard_map/ppermute | solution.py:316
  58.5 16.4 %collective-permute-start.15 = (bf16[128,3200]{1,0:T(8,128)(2,1)S(1)}, bf16[128,3200]{1,0:T(8,128)(2,1)S(1)}, u32[]{:S(2)}, u32[]{:S(2)}) collective-permute-start(bf16[128,3200]{1,0:T(8,128)(2,1)S(1)} %concatenate.6.refs_0_), channel_id=1, source_target_pairs={{0,2},{2,0},{4,6},{6,4},{8,10},{10,8},{12,14},{14,12},{16,18},{18,... | collective-permute-start | bytes 2457608 | tf_op jit(solution)/shard_map/ppermute | solution.py:305
  58.5 17.6 %collective-permute-start.16 = (bf16[128,3200]{1,0:T(8,128)(2,1)}, bf16[128,3200]{1,0:T(8,128)(2,1)S(1)}, u32[]{:S(2)}, u32[]{:S(2)}) collective-permute-start(bf16[128,3200]{1,0:T(8,128)(2,1)} %copy-done.4), channel_id=1, source_target_pairs={{0,2},{2,0},{4,6},{6,4},{8,10},{10,8},{12,14},{14,12},{16,18},{18,... | collective-permute-start | bytes 2457608 | tf_op jit(solution)/shard_map/ppermute | solution.py:305
  76.1 23.2 %collective-permute-start.10 = (bf16[128,3200]{1,0:T(8,128)(2,1)S(1)}, bf16[128,3200]{1,0:T(8,128)(2,1)S(1)}, u32[]{:S(2)}, u32[]{:S(2)}) collective-permute-start(bf16[128,3200]{1,0:T(8,128)(2,1)S(1)} %broadcast_select_fusion.refs_8_), channel_id=1, source_target_pairs={{0,4},{2,6},{4,0},{6,2},{8,12},{10,14},{12,8},{14,10},{16,20},{18,... | collective-permute-start | bytes 2457608 | tf_op jit(solution)/shard_map/ppermute | solution.py:305
  76.7 22.6 %collective-permute-start.14 = (bf16[128,3200]{1,0:T(8,128)(2,1)S(1)}, bf16[128,3200]{1,0:T(8,128)(2,1)S(1)}, u32[]{:S(2)}, u32[]{:S(2)}) collective-permute-start(bf16[128,3200]{1,0:T(8,128)(2,1)S(1)} %broadcast_select_fusion.refs_8_), channel_id=1, source_target_pairs={{0,2},{2,0},{4,6},{6,4},{8,10},{10,8},{12,14},{14,12},{16,18},{18,... | collective-permute-start | bytes 2457608 | tf_op jit(solution)/shard_map/ppermute | solution.py:305
  76.9 22.5 %collective-permute-start.12 = (bf16[128,3200]{1,0:T(8,128)(2,1)S(1)}, bf16[128,3200]{1,0:T(8,128)(2,1)S(1)}, u32[]{:S(2)}, u32[]{:S(2)}) collective-permute-start(bf16[128,3200]{1,0:T(8,128)(2,1)S(1)} %broadcast_select_fusion.1.refs_0_), channel_id=1, source_target_pairs={{0,2},{2,0},{4,6},{6,4},{8,10},{10,8},{12,14},{14,12},{16,18},{18,... | collective-permute-start | bytes 2457608 | tf_op jit(solution)/shard_map/ppermute | solution.py:305
  77.2 22.1 %collective-permute-start.13 = (bf16[128,3200]{1,0:T(8,128)(2,1)}, bf16[128,3200]{1,0:T(8,128)(2,1)S(1)}, u32[]{:S(2)}, u32[]{:S(2)}) collective-permute-start(bf16[128,3200]{1,0:T(8,128)(2,1)} %collective-permute-done.8.refs_1_), channel_id=1, source_target_pairs={{0,2},{2,0},{4,6},{6,4},{8,10},{10,8},{12,14},{14,12},{16,18},{18,... | collective-permute-start | bytes 2457608 | tf_op jit(solution)/shard_map/ppermute | solution.py:305
  77.5 21.8 %collective-permute-start.11 = (bf16[3,128,1024]{2,1,0:T(8,128)(2,1)S(1)}, bf16[3,128,1024]{2,1,0:T(8,128)(2,1)S(1)}, u32[]{:S(2)}, u32[]{:S(2)}) collective-permute-start(bf16[3,128,1024]{2,1,0:T(8,128)(2,1)S(1)} %pad_maximum_fusion), channel_id=1, source_target_pairs={{0,1},{1,0},{2,3},{3,2},{4,5},{5,4},{6,7},{7,6},{8,9},{9,8},{10,11... | collective-permute-start | bytes 2359304 | tf_op jit(solution)/shard_map/ppermute | solution.py:316
  113.1 25.3 %collective-permute-start.25 = (bf16[4,128,1024]{2,1,0:T(8,128)(2,1)S(1)}, bf16[4,128,1024]{2,1,0:T(8,128)(2,1)S(1)}, u32[]{:S(2)}, u32[]{:S(2)}) collective-permute-start(bf16[4,128,1024]{2,1,0:T(8,128)(2,1)S(1)} %get-tuple-element.165), channel_id=1, source_target_pairs={{0,1},{1,0},{2,3},{3,2},{4,5},{5,4},{6,7},{7,6},{8,9},{9,8},{10,11... | collective-permute-start | bytes 3145736 | tf_op jit(solution)/shard_map/ppermute | solution.py:316
  113.7 24.9 %collective-permute-start.26 = (bf16[4,128,1024]{2,1,0:T(8,128)(2,1)S(1)}, bf16[4,128,1024]{2,1,0:T(8,128)(2,1)S(1)}, u32[]{:S(2)}, u32[]{:S(2)}) collective-permute-start(bf16[4,128,1024]{2,1,0:T(8,128)(2,1)S(1)} %get-tuple-element.164), channel_id=1, source_target_pairs={{0,4},{2,6},{4,0},{6,2},{8,12},{10,14},{12,8},{14,10},{16,20},{18,... | collective-permute-start | bytes 3145736 | tf_op jit(solution)/shard_map/ppermute | solution.py:305
  138.6 13.0 %collective-permute-start.33 = (bf16[8,128,1024]{2,1,0:T(8,128)(2,1)}, bf16[8,128,1024]{2,1,0:T(8,128)(2,1)}, u32[]{:S(2)}, u32[]{:S(2)}) collective-permute-start(bf16[8,128,1024]{2,1,0:T(8,128)(2,1)} %get-tuple-element.129), channel_id=1, source_target_pairs={{0,2},{2,0},{4,6},{6,4},{8,10},{10,8},{12,14},{14,12},{16,18},{18,... | collective-permute-start | bytes 6291464 | tf_op jit(solution)/shard_map/ppermute | solution.py:305
  142.2 15.2 %collective-permute-start.31 = (bf16[2,128,1024]{2,1,0:T(8,128)(2,1)}, bf16[2,128,1024]{2,1,0:T(8,128)(2,1)}, u32[]{:S(2)}, u32[]{:S(2)}) collective-permute-start(bf16[2,128,1024]{2,1,0:T(8,128)(2,1)} %get-tuple-element.163), channel_id=1, source_target_pairs={{0,4},{2,6},{4,0},{6,2},{8,12},{10,14},{12,8},{14,10},{16,20},{18,... | collective-permute-start | bytes 1572872 | tf_op jit(solution)/shard_map/ppermute | solution.py:305
  143.7 15.1 %collective-permute-start.32 = (bf16[2,128,1024]{2,1,0:T(8,128)(2,1)}, bf16[2,128,1024]{2,1,0:T(8,128)(2,1)}, u32[]{:S(2)}, u32[]{:S(2)}) collective-permute-start(bf16[2,128,1024]{2,1,0:T(8,128)(2,1)} %get-tuple-element.162), channel_id=1, source_target_pairs={{0,1},{1,0},{2,3},{3,2},{4,5},{5,4},{6,7},{7,6},{8,9},{9,8},{10,11... | collective-permute-start | bytes 1572872 | tf_op jit(solution)/shard_map/ppermute | solution.py:316
  147.3 22.7 %collective-permute-start.29 = (bf16[2,128,1024]{2,1,0:T(8,128)(2,1)}, bf16[2,128,1024]{2,1,0:T(8,128)(2,1)}, u32[]{:S(2)}, u32[]{:S(2)}) collective-permute-start(bf16[2,128,1024]{2,1,0:T(8,128)(2,1)} %get-tuple-element.177), channel_id=1, source_target_pairs={{0,1},{1,0},{2,3},{3,2},{4,5},{5,4},{6,7},{7,6},{8,9},{9,8},{10,11... | collective-permute-start | bytes 1572872 | tf_op jit(solution)/shard_map/ppermute | solution.py:316
  148.9 21.2 %collective-permute-start.30 = (bf16[2,128,1024]{2,1,0:T(8,128)(2,1)}, bf16[2,128,1024]{2,1,0:T(8,128)(2,1)}, u32[]{:S(2)}, u32[]{:S(2)}) collective-permute-start(bf16[2,128,1024]{2,1,0:T(8,128)(2,1)} %get-tuple-element.176), channel_id=1, source_target_pairs={{0,4},{2,6},{4,0},{6,2},{8,12},{10,14},{12,8},{14,10},{16,20},{18,... | collective-permute-start | bytes 1572872 | tf_op jit(solution)/shard_map/ppermute | solution.py:305
  153.4 30.5 %collective-permute-start.34 = (bf16[2,128,1024]{2,1,0:T(8,128)(2,1)S(1)}, bf16[2,128,1024]{2,1,0:T(8,128)(2,1)S(1)}, u32[]{:S(2)}, u32[]{:S(2)}) collective-permute-start(bf16[2,128,1024]{2,1,0:T(8,128)(2,1)S(1)} %get-tuple-element.175), channel_id=1, source_target_pairs={{0,1},{1,0},{2,3},{3,2},{4,5},{5,4},{6,7},{7,6},{8,9},{9,8},{10,11... | collective-permute-start | bytes 1572872 | tf_op jit(solution)/shard_map/ppermute | solution.py:316
  157.3 26.7 %collective-permute-start.35 = (bf16[2,128,1024]{2,1,0:T(8,128)(2,1)S(1)}, bf16[2,128,1024]{2,1,0:T(8,128)(2,1)S(1)}, u32[]{:S(2)}, u32[]{:S(2)}) collective-permute-start(bf16[2,128,1024]{2,1,0:T(8,128)(2,1)S(1)} %get-tuple-element.174), channel_id=1, source_target_pairs={{0,4},{2,6},{4,0},{6,2},{8,12},{10,14},{12,8},{14,10},{16,20},{18,... | collective-permute-start | bytes 1572872 | tf_op jit(solution)/shard_map/ppermute | solution.py:305
  173.2 12.4 %collective-permute-start.38 = (bf16[2,128,1024]{2,1,0:T(8,128)(2,1)S(1)}, bf16[2,128,1024]{2,1,0:T(8,128)(2,1)S(1)}, u32[]{:S(2)}, u32[]{:S(2)}) collective-permute-start(bf16[2,128,1024]{2,1,0:T(8,128)(2,1)S(1)} %pad_maximum_fusion.3), channel_id=1, source_target_pairs={{0,8},{2,10},{4,12},{6,14},{8,0},{10,2},{12,4},{14,6},{16,24},{18,... | collective-permute-start | bytes 1572872 | tf_op jit(solution)/shard_map/ppermute | solution.py:305
  187.2 14.7 %collective-permute-start.41 = (bf16[2,128,1024]{2,1,0:T(8,128)(2,1)S(1)}, bf16[2,128,1024]{2,1,0:T(8,128)(2,1)S(1)}, u32[]{:S(2)}, u32[]{:S(2)}) collective-permute-start(bf16[2,128,1024]{2,1,0:T(8,128)(2,1)S(1)} %pad_maximum_fusion.4), channel_id=1, source_target_pairs={{0,8},{2,10},{4,12},{6,14},{24,16},{26,18},{28,20},{30,22},{8,24},... | collective-permute-start | bytes 1572872 | tf_op jit(solution)/shard_map/ppermute | solution.py:305
  189.6 12.3 %collective-permute-start.39 = (bf16[128,1024]{1,0:T(8,128)(2,1)S(1)}, bf16[128,1024]{1,0:T(8,128)(2,1)S(1)}, u32[]{:S(2)}, u32[]{:S(2)}) collective-permute-start(bf16[128,1024]{1,0:T(8,128)(2,1)S(1)} %get-tuple-element.171), channel_id=1, source_target_pairs={{0,4},{2,6},{4,0},{6,2},{8,12},{10,14},{12,8},{14,10},{16,20},{18,... | collective-permute-start | bytes 786440 | tf_op jit(solution)/shard_map/ppermute | solution.py:305
  191.2 10.7 %collective-permute-start.40 = (bf16[128,1024]{1,0:T(8,128)(2,1)S(1)}, bf16[128,1024]{1,0:T(8,128)(2,1)S(1)}, u32[]{:S(2)}, u32[]{:S(2)}) collective-permute-start(bf16[128,1024]{1,0:T(8,128)(2,1)S(1)} %get-tuple-element.170), channel_id=1, source_target_pairs={{0,1},{1,0},{2,3},{3,2},{4,5},{5,4},{6,7},{7,6},{8,9},{9,8},{10,11... | collective-permute-start | bytes 786440 | tf_op jit(solution)/shard_map/ppermute | solution.py:316
  203.7 27.1 %collective-permute-start.43 = (bf16[2,128,1024]{2,1,0:T(8,128)(2,1)S(1)}, bf16[2,128,1024]{2,1,0:T(8,128)(2,1)S(1)}, u32[]{:S(2)}, u32[]{:S(2)}) collective-permute-start(bf16[2,128,1024]{2,1,0:T(8,128)(2,1)S(1)} %fusion), channel_id=1, source_target_pairs={{8,16},{10,18},{12,20},{14,22},{16,8},{18,10},{20,12},{22,14},{9,1... | collective-permute-start | bytes 1572872 | tf_op jit(solution)/shard_map/ppermute | solution.py:305
  206.2 24.6 %collective-permute-start.42 = (bf16[2,128,1024]{2,1,0:T(8,128)(2,1)S(1)}, bf16[2,128,1024]{2,1,0:T(8,128)(2,1)S(1)}, u32[]{:S(2)}, u32[]{:S(2)}) collective-permute-start(bf16[2,128,1024]{2,1,0:T(8,128)(2,1)S(1)} %pad_maximum_fusion.5), channel_id=1, source_target_pairs={{0,24},{2,26},{4,28},{6,30},{24,0},{26,2},{28,4},{30,6},{1,25},{3,... | collective-permute-start | bytes 1572872 | tf_op jit(solution)/shard_map/ppermute | solution.py:305
  (33 other events, 321.9 us)

commit v3 on v2

--- a/solution.py
+++ b/solution.py
@@ -392,10 +392,11 @@
     gps = jnp.concatenate([gp_a[:local], gp_b[:local]], axis=1).reshape(local, 4, 4, rows)
     gps = gps[:, :, jnp.array([0, 2, 1, 3])].reshape(local, owners, rows).transpose(1, 0, 2)
     gps = gps[jnp.arange(owners) ^ place]
-    one_2, two_a, gps = sync((one_2, two_a, gps))
+    sum1 = layer_sum(keep_a, got_a, one_a, two_a, 1).astype(BF)
+    one_2, two_a, gps, sum1 = sync((one_2, two_a, gps, sum1))
 
     one_3, two_2 = first_sums(keep3, got3), second_sums(keep2, got2, one_2)
-    from1 = over_z(layer_sum(keep_a, got_a, one_a, two_a, 1).astype(BF))
+    from1 = over_z(sum1)
     grad_gate, grad_up = weight_grads([xs_a, xs_b], [hs_a, hs_b], hid, 2 * hid, 2, w_gate.shape, "grad_in")
     one_3, two_2, from1, grad_gate, grad_up = sync((one_3, two_2, from1, grad_gate, grad_up))
 

time: 236 us -> 234 us (level)
  other arithmetic: 24.9 us -> 22.2 us
    ppermute x11, starting transfers between devices: 12.1 us -> 14.9 us  [over_y(): return lax.ppermute(v, 'col', [(0, 1), (1, 0)])]
    ppermute x34, starting transfers between devices: 34.5 us -> 31.8 us  [permute(): return lambda v: lax.ppermute(v, 'dp', pairs)]
  transfers between devices with their start and end apart: 45 -> 45, of which waited for: 20 -> 22; matrix products, arithmetic and copies ran while one was open for 8% -> 7% of each run, Pallas kernels for 22% -> 22%
where the time goes in v3:
time: 234 us; the launch traced here: 231 us
  waiting for transfers between devices  93 us (40%)
  Pallas kernels  51.3 us (22%)
  starting transfers between devices  46.8 us (20%)
  other arithmetic  22.2 us (9%)
  blocking collectives  11.1 us (5%)
  local copies, waits for them, and re-layouts  4.79 us (2%)
    ppermute x34, waiting for transfers between devices, permute(): return lambda v: lax.ppermute(v, 'dp', pairs)  52.6 us
    ppermute x11, waiting for transfers between devices, over_y(): return lax.ppermute(v, 'col', [(0, 1), (1, 0)])  40.4 us
    pallas_call x2, Pallas kernels, rounds(): pl.pallas_call(functools.partial(rounds_kernel, cap, count, index, split)...  39.8 us
    ppermute x34, starting transfers between devices, permute(): return lambda v: lax.ppermute(v, 'dp', pairs)  31.8 us
    ppermute x11, starting transfers between devices, over_y(): return lax.ppermute(v, 'col', [(0, 1), (1, 0)])  14.9 us
    convert_element_type x8, other arithmetic, add16(): return add(*terms).astype(BF)  11.7 us
    pallas_call x2, Pallas kernels, weight_grads(): pl.pallas_call(functools.partial(weight_kernel, rounds, off, outs_n), in_...  11.4 us
    all_to_all x1, blocking collectives, body16(): back = lax.all_to_all(gps, 'dp', 0, 0, tiled=True)  11.1 us
  transfers between devices with their start and end apart: 45, of which 22 were waited for; matrix products, arithmetic and copies ran while one was open for 7% of the time, Pallas kernels for 22%

profile of v3, /device:TPU:8, one launch (start us, length us, event | category | flops | bytes accessed | tf_op | source)
XLA Modules:
  0.0 230.5 jit_solution(12636913267090297509)
XLA Ops:
  3.0 5.0 %collective-permute-start.1 = (bf16[128,3200]{1,0:T(8,128)(2,1)S(1)}, bf16[128,3200]{1,0:T(8,128)(2,1)}, u32[]{:S(2)}, u32[]{:S(2)}) collective-permute-start(bf16[128,3200]{1,0:T(8,128)(2,1)S(1)} %concatenate.6.refs_0_), channel_id=1, source_target_pairs={{8,16},{10,18},{12,20},{14,22},{16,8},{18,10},{20,12},{22,14},{9,1... | collective-permute-start | bytes 2457608 | tf_op jit(solution)/shard_map/ppermute | solution.py:305
  9.6 13.4 %collective-permute-done.refs_8_ = bf16[128,3200]{1,0:T(8,128)(2,1)S(1)} collective-permute-done((bf16[128,3200]{1,0:T(8,128)(2,1)S(1)}, bf16[128,3200]{1,0:T(8,128)(2,1)S(1)}, u32[]{:S(2)}, u32[]{:S(2)}) %collective-permute-start) | collective-permute-done | bytes 819232 | tf_op jit(solution)/shard_map/ppermute | solution.py:305
  22.9 3.1 %collective-permute-done.1 = bf16[128,3200]{1,0:T(8,128)(2,1)} collective-permute-done((bf16[128,3200]{1,0:T(8,128)(2,1)S(1)}, bf16[128,3200]{1,0:T(8,128)(2,1)}, u32[]{:S(2)}, u32[]{:S(2)}) %collective-permute-start.1) | collective-permute-done | bytes 819232 | tf_op jit(solution)/shard_map/ppermute | solution.py:305
  27.5 2.2 collective-permute-start.4
  29.7 1.6 collective-permute-start.5
  31.3 2.2 collective-permute-start.3
  33.6 1.6 collective-permute-start.6
  35.2 10.5 %collective-permute-done.6.refs_4_.refs_5_ = bf16[2,128,1024]{2,1,0:T(8,128)(2,1)S(1)} collective-permute-done((bf16[2,128,1024]{2,1,0:T(8,128)(2,1)S(1)}, bf16[2,128,1024]{2,1,0:T(8,128)(2,1)S(1)}, u32[]{:S(2)}, u32[]{:S(2)}) %collective-permute-start.6) | collective-permute-done | bytes 524320 | tf_op jit(solution)/shard_map/ppermute | solution.py:316
  45.6 2.4 %collective-permute-done.4 = bf16[128,3200]{1,0:T(8,128)(2,1)} collective-permute-done((bf16[128,3200]{1,0:T(8,128)(2,1)S(1)}, bf16[128,3200]{1,0:T(8,128)(2,1)}, u32[]{:S(2)}, u32[]{:S(2)}) %collective-permute-start.4) | collective-permute-done | bytes 819232 | tf_op jit(solution)/shard_map/ppermute | solution.py:305
  49.0 5.3 %collective-permute-start.7 = (bf16[128,3200]{1,0:T(8,128)(2,1)}, bf16[128,3200]{1,0:T(8,128)(2,1)}, u32[]{:S(2)}, u32[]{:S(2)}) collective-permute-start(bf16[128,3200]{1,0:T(8,128)(2,1)} %collective-permute-done.4), channel_id=1, source_target_pairs={{8,0},{10,2},{12,4},{14,6},{16,24},{18,26},{20,28},{22,30},{9,1},{... | collective-permute-start | bytes 2457608 | tf_op jit(solution)/shard_map/ppermute | solution.py:305
  59.1 9.1 %collective-permute-done.9.refs_12_.refs_13_ = bf16[2,128,1024]{2,1,0:T(8,128)(2,1)} collective-permute-done((bf16[2,128,1024]{2,1,0:T(8,128)(2,1)}, bf16[2,128,1024]{2,1,0:T(8,128)(2,1)}, u32[]{:S(2)}, u32[]{:S(2)}) %collective-permute-start.9) | collective-permute-done | bytes 524320 | tf_op jit(solution)/shard_map/ppermute | solution.py:316
  68.2 5.0 %collective-permute-done.8.refs_1_ = bf16[128,3200]{1,0:T(8,128)(2,1)} collective-permute-done((bf16[128,3200]{1,0:T(8,128)(2,1)S(1)}, bf16[128,3200]{1,0:T(8,128)(2,1)}, u32[]{:S(2)}, u32[]{:S(2)}) %collective-permute-start.8) | collective-permute-done | bytes 819232 | tf_op jit(solution)/shard_map/ppermute | solution.py:305
  77.5 1.6 collective-permute-start.11
  79.2 20.1 %moe_rounds.2 = (bf16[2,384,2048]{2,1,0:T(8,128)(2,1)}, bf16[2,384,2048]{2,1,0:T(8,128)(2,1)}, bf16[2,384,1152]{2,1,0:T(8,128)(2,1)}, f32[8,1024]{1,0:T(8,128)S(...) custom-call(s32[2]{0:T(128)S(1)} %pad_add_fusion.at_ref, bf16[128,3200]{1,0:T(8,128)(2,1)S(1)} %concatenate.6.refs_0_, ...), custom_call_target="tpu_custom_call" | custom-call | flops 7247757312 | bytes 34603008 | tf_op jit(solution)/shard_map/moe_rounds/pallas_call | solution.py:182
  100.6 8.1 %collective-permute-done.21.refs_13_ = bf16[1,128,1024]{2,1,0:T(8,128)(2,1)S(1)} collective-permute-done((bf16[1,128,1024]{2,1,0:T(8,128)(2,1)S(1)}, bf16[1,128,1024]{2,1,0:T(8,128)(2,1)S(1)}, u32[]{:S(2)}, u32[]{:S(2)}) %collective-permute-start.21) | collective-permute-done | bytes 262176 | tf_op jit(solution)/shard_map/ppermute | solution.py:316
  109.1 4.0 %add_convert_fusion = (bf16[4,128,1024]{2,1,0:T(8,128)(2,1)S(1)}, bf16[4,128,1024]{2,1,0:T(8,128)(2,1)S(1)}) fusion(bf16[16,128,1024]{2,1,0:T(8,128)(2,1)S(1)} %collective-permute-done.24, bf16[16,128,1024]{2,1,0:T(8,128)(2,1)} %get-tuple-element.104), kind=kLoop, calls=%fused_computation.2 | loop fusion | flops 4194304 | bytes 6291456 | tf_op jit(solution)/shard_map/convert_element_type | solution.py:290
  116.7 19.7 %moe_rounds.3 = (bf16[2,384,2048]{2,1,0:T(8,128)(2,1)}, bf16[2,384,2048]{2,1,0:T(8,128)(2,1)}, bf16[2,384,1152]{2,1,0:T(8,128)(2,1)}, f32[8,1024]{1,0:T(8,128)S(...) custom-call(s32[2]{0:T(128)S(1)} %pad_add_fusion.at_ref, ...), custom_call_target="tpu_custom_call" | custom-call | flops 7247757312 | bytes 34603008 | tf_op jit(solution)/shard_map/moe_rounds/pallas_call | solution.py:182
  136.4 2.0 collective-permute-done.25
  139.1 2.9 %add_convert_fusion.4 = (bf16[2,128,1024]{2,1,0:T(8,128)(2,1)}, bf16[2,128,1024]{2,1,0:T(8,128)(2,1)}) fusion(bf16[4,128,1024]{2,1,0:T(8,128)(2,1)S(1)} %collective-permute-done.26, bf16[16,128,1024]{2,1,0:T(8,128)(2,1)S(1)} %collective-permute-done.24, bf16[16,128,1024]{2,1,0:T(8,128)(2,1)} %get-tuple-element.104, ...), kind=kLoop, calls=%fused_computation.13 | loop fusion | flops 3145728 | bytes 4194304 | tf_op jit(solution)/shard_map/convert_element_type | solution.py:290
  146.3 2.0 add_convert_fusion.6
  151.2 5.8 %collective-permute-done.31 = bf16[2,128,1024]{2,1,0:T(8,128)(2,1)S(1)} collective-permute-done((bf16[2,128,1024]{2,1,0:T(8,128)(2,1)}, bf16[2,128,1024]{2,1,0:T(8,128)(2,1)S(1)}, u32[]{:S(2)}, u32[]{:S(2)}) %collective-permute-start.31) | collective-permute-done | bytes 524320 | tf_op jit(solution)/shard_map/ppermute | solution.py:305
  158.5 1.9 add_convert_fusion.13
  160.9 1.6 collective-permute-start.34
  163.0 6.7 %collective-permute-done.29 = bf16[2,128,1024]{2,1,0:T(8,128)(2,1)S(1)} collective-permute-done((bf16[2,128,1024]{2,1,0:T(8,128)(2,1)S(1)}, bf16[2,128,1024]{2,1,0:T(8,128)(2,1)S(1)}, u32[]{:S(2)}, u32[]{:S(2)}) %collective-permute-start.29) | collective-permute-done | bytes 524320 | tf_op jit(solution)/shard_map/ppermute | solution.py:316
  173.4 7.0 %grad_in.1 = (bf16[2,2048,384]{2,1,0:T(8,128)(2,1)}, bf16[2,2048,384]{2,1,0:T(8,128)(2,1)}) custom-call(bf16[2,384,2048]{2,1,0:T(8,128)(2,1)S(1)} %copy-done.9, bf16[2,384,2048]{2,1,0:T(8,128)(2,1)S(1)} %copy-done.8, bf16[2,384,1152]{2,1,0:T(8,128)(2,1)S(1)} %copy-done.2, bf16[2,384,1152]{2,1,0:T(8,128)(2,1)S(1)} %copy-done.3), custom_call_target="tpu_custom_call" | custom-call | flops 4831838208 | bytes 14942208 | tf_op jit(solution)/shard_map/grad_in/pallas_call | solution.py:256
  181.0 3.1 %collective-permute-done.36 = bf16[128,1024]{1,0:T(8,128)(2,1)S(1)} collective-permute-done((bf16[128,1024]{1,0:T(8,128)(2,1)S(1)}, bf16[128,1024]{1,0:T(8,128)(2,1)S(1)}, u32[]{:S(2)}, u32[]{:S(2)}) %collective-permute-start.36) | collective-permute-done | bytes 262176 | tf_op jit(solution)/shard_map/ppermute | solution.py:305
  189.4 11.1 %all_to_all.5 = f32[16,2,128]{2,1,0:T(2,128)S(1)} all-to-all(f32[16,2,128]{2,1,0:T(2,128)S(1)} %gather_fusion.1), channel_id=1, replica_groups=mesh['dp'=16,'col'=2] {'dp'}, dimensions={0} | all-to-all | bytes 32768 | tf_op jit(solution)/shard_map/all_to_all | solution.py:405
  201.2 2.9 %collective-permute-start.43 = (bf16[2,128,1024]{2,1,0:T(8,128)(2,1)S(1)}, bf16[2,128,1024]{2,1,0:T(8,128)(2,1)S(1)}, u32[]{:S(2)}, u32[]{:S(2)}) collective-permute-start(bf16[2,128,1024]{2,1,0:T(8,128)(2,1)S(1)} %fusion), channel_id=1, source_target_pairs={{8,16},{10,18},{12,20},{14,22},{16,8},{18,10},{20,12},{22,14},{9,1... | collective-permute-start | bytes 1572872 | tf_op jit(solution)/shard_map/ppermute | solution.py:305
  204.7 4.5 %grad_down.1 = bf16[2,384,2048]{2,1,0:T(8,128)(2,1)} custom-call(bf16[2,384,2048]{2,1,0:T(8,128)(2,1)S(1)} %copy-done, bf16[2,384,2048]{2,1,0:T(8,128)(2,1)S(1)} %copy-done.1, bf16[2,384,1152]{2,1,0:T(8,128)(2,1)S(1)} %copy-done.2, bf16[2,384,1152]{2,1,0:T(8,128)(2,1)S(1)} %copy-done.3), custom_call_target="tpu_custom_call" | custom-call | flops 2415919104 | bytes 10616832 | tf_op jit(solution)/shard_map/grad_down/pallas_call | solution.py:256
  209.3 1.6 collective-permute-start.44
  210.8 1.7 convert_add_fusion.3
  213.1 15.3 %collective-permute-done.43 = bf16[2,128,1024]{2,1,0:T(8,128)(2,1)S(1)} collective-permute-done((bf16[2,128,1024]{2,1,0:T(8,128)(2,1)S(1)}, bf16[2,128,1024]{2,1,0:T(8,128)(2,1)S(1)}, u32[]{:S(2)}, u32[]{:S(2)}) %collective-permute-start.43) | collective-permute-done | bytes 524320 | tf_op jit(solution)/shard_map/ppermute | solution.py:305
  (145 shorter events, 44.2 us)
Async XLA Ops:
  2.9 20.0 %collective-permute-start = (bf16[128,3200]{1,0:T(8,128)(2,1)S(1)}, bf16[128,3200]{1,0:T(8,128)(2,1)S(1)}, u32[]{:S(2)}, u32[]{:S(2)}) collective-permute-start(bf16[128,3200]{1,0:T(8,128)(2,1)S(1)} %concatenate.6.refs_0_), channel_id=1, source_target_pairs={{0,8},{2,10},{4,12},{6,14},{8,0},{10,2},{12,4},{14,6},{16,24},{18,... | collective-permute-start | bytes 2457608 | tf_op jit(solution)/shard_map/ppermute | solution.py:305
  3.0 23.1 %collective-permute-start.1 = (bf16[128,3200]{1,0:T(8,128)(2,1)S(1)}, bf16[128,3200]{1,0:T(8,128)(2,1)}, u32[]{:S(2)}, u32[]{:S(2)}) collective-permute-start(bf16[128,3200]{1,0:T(8,128)(2,1)S(1)} %concatenate.6.refs_0_), channel_id=1, source_target_pairs={{8,16},{10,18},{12,20},{14,22},{16,8},{18,10},{20,12},{22,14},{9,1... | collective-permute-start | bytes 2457608 | tf_op jit(solution)/shard_map/ppermute | solution.py:305
  8.0 19.5 %collective-permute-start.2 = (bf16[128,3200]{1,0:T(8,128)(2,1)S(1)}, bf16[128,3200]{1,0:T(8,128)(2,1)S(1)}, u32[]{:S(2)}, u32[]{:S(2)}) collective-permute-start(bf16[128,3200]{1,0:T(8,128)(2,1)S(1)} %concatenate.6.refs_0_), channel_id=1, source_target_pairs={{0,4},{2,6},{4,0},{6,2},{8,12},{10,14},{12,8},{14,10},{16,20},{18,... | collective-permute-start | bytes 2457608 | tf_op jit(solution)/shard_map/ppermute | solution.py:305
  27.5 20.6 %collective-permute-start.4 = (bf16[128,3200]{1,0:T(8,128)(2,1)S(1)}, bf16[128,3200]{1,0:T(8,128)(2,1)}, u32[]{:S(2)}, u32[]{:S(2)}) collective-permute-start(bf16[128,3200]{1,0:T(8,128)(2,1)S(1)} %collective-permute-done.refs_8_), channel_id=1, source_target_pairs={{8,16},{10,18},{12,20},{14,22},{16,8},{18,10},{20,12},{22,14},{9,1... | collective-permute-start | bytes 2457608 | tf_op jit(solution)/shard_map/ppermute | solution.py:305
  29.7 18.7 %collective-permute-start.5 = (bf16[128,3200]{1,0:T(8,128)(2,1)S(1)}, bf16[128,3200]{1,0:T(8,128)(2,1)S(1)}, u32[]{:S(2)}, u32[]{:S(2)}) collective-permute-start(bf16[128,3200]{1,0:T(8,128)(2,1)S(1)} %collective-permute-done.refs_8_), channel_id=1, source_target_pairs={{0,4},{2,6},{4,0},{6,2},{8,12},{10,14},{12,8},{14,10},{16,20},{18,... | collective-permute-start | bytes 2457608 | tf_op jit(solution)/shard_map/ppermute | solution.py:305
  31.3 17.7 %collective-permute-start.3 = (bf16[128,3200]{1,0:T(8,128)(2,1)}, bf16[128,3200]{1,0:T(8,128)(2,1)}, u32[]{:S(2)}, u32[]{:S(2)}) collective-permute-start(bf16[128,3200]{1,0:T(8,128)(2,1)} %collective-permute-done.1), channel_id=1, source_target_pairs={{8,0},{10,2},{12,4},{14,6},{16,24},{18,26},{20,28},{22,30},{9,1},{... | collective-permute-start | bytes 2457608 | tf_op jit(solution)/shard_map/ppermute | solution.py:305
  49.0 24.1 %collective-permute-start.7 = (bf16[128,3200]{1,0:T(8,128)(2,1)}, bf16[128,3200]{1,0:T(8,128)(2,1)}, u32[]{:S(2)}, u32[]{:S(2)}) collective-permute-start(bf16[128,3200]{1,0:T(8,128)(2,1)} %collective-permute-done.4), channel_id=1, source_target_pairs={{8,0},{10,2},{12,4},{14,6},{16,24},{18,26},{20,28},{22,30},{9,1},{... | collective-permute-start | bytes 2457608 | tf_op jit(solution)/shard_map/ppermute | solution.py:305
  55.6 17.6 %collective-permute-start.8 = (bf16[128,3200]{1,0:T(8,128)(2,1)S(1)}, bf16[128,3200]{1,0:T(8,128)(2,1)}, u32[]{:S(2)}, u32[]{:S(2)}) collective-permute-start(bf16[128,3200]{1,0:T(8,128)(2,1)S(1)} %broadcast_select_fusion.1.refs_0_), channel_id=1, source_target_pairs={{0,4},{2,6},{4,0},{6,2},{8,12},{10,14},{12,8},{14,10},{16,20},{18,... | collective-permute-start | bytes 2457608 | tf_op jit(solution)/shard_map/ppermute | solution.py:305
  58.6 16.4 %collective-permute-start.15 = (bf16[128,3200]{1,0:T(8,128)(2,1)S(1)}, bf16[128,3200]{1,0:T(8,128)(2,1)S(1)}, u32[]{:S(2)}, u32[]{:S(2)}) collective-permute-start(bf16[128,3200]{1,0:T(8,128)(2,1)S(1)} %concatenate.6.refs_0_), channel_id=1, source_target_pairs={{0,2},{2,0},{4,6},{6,4},{8,10},{10,8},{12,14},{14,12},{16,18},{18,... | collective-permute-start | bytes 2457608 | tf_op jit(solution)/shard_map/ppermute | solution.py:305
  58.6 17.6 %collective-permute-start.16 = (bf16[128,3200]{1,0:T(8,128)(2,1)}, bf16[128,3200]{1,0:T(8,128)(2,1)S(1)}, u32[]{:S(2)}, u32[]{:S(2)}) collective-permute-start(bf16[128,3200]{1,0:T(8,128)(2,1)} %copy-done.4), channel_id=1, source_target_pairs={{0,2},{2,0},{4,6},{6,4},{8,10},{10,8},{12,14},{14,12},{16,18},{18,... | collective-permute-start | bytes 2457608 | tf_op jit(solution)/shard_map/ppermute | solution.py:305
  76.1 23.2 %collective-permute-start.10 = (bf16[128,3200]{1,0:T(8,128)(2,1)S(1)}, bf16[128,3200]{1,0:T(8,128)(2,1)S(1)}, u32[]{:S(2)}, u32[]{:S(2)}) collective-permute-start(bf16[128,3200]{1,0:T(8,128)(2,1)S(1)} %broadcast_select_fusion.refs_8_), channel_id=1, source_target_pairs={{0,4},{2,6},{4,0},{6,2},{8,12},{10,14},{12,8},{14,10},{16,20},{18,... | collective-permute-start | bytes 2457608 | tf_op jit(solution)/shard_map/ppermute | solution.py:305
  76.7 22.6 %collective-permute-start.14 = (bf16[128,3200]{1,0:T(8,128)(2,1)S(1)}, bf16[128,3200]{1,0:T(8,128)(2,1)S(1)}, u32[]{:S(2)}, u32[]{:S(2)}) collective-permute-start(bf16[128,3200]{1,0:T(8,128)(2,1)S(1)} %broadcast_select_fusion.refs_8_), channel_id=1, source_target_pairs={{0,2},{2,0},{4,6},{6,4},{8,10},{10,8},{12,14},{14,12},{16,18},{18,... | collective-permute-start | bytes 2457608 | tf_op jit(solution)/shard_map/ppermute | solution.py:305
  76.9 22.5 %collective-permute-start.12 = (bf16[128,3200]{1,0:T(8,128)(2,1)S(1)}, bf16[128,3200]{1,0:T(8,128)(2,1)S(1)}, u32[]{:S(2)}, u32[]{:S(2)}) collective-permute-start(bf16[128,3200]{1,0:T(8,128)(2,1)S(1)} %broadcast_select_fusion.1.refs_0_), channel_id=1, source_target_pairs={{0,2},{2,0},{4,6},{6,4},{8,10},{10,8},{12,14},{14,12},{16,18},{18,... | collective-permute-start | bytes 2457608 | tf_op jit(solution)/shard_map/ppermute | solution.py:305
  77.2 22.1 %collective-permute-start.13 = (bf16[128,3200]{1,0:T(8,128)(2,1)}, bf16[128,3200]{1,0:T(8,128)(2,1)S(1)}, u32[]{:S(2)}, u32[]{:S(2)}) collective-permute-start(bf16[128,3200]{1,0:T(8,128)(2,1)} %collective-permute-done.8.refs_1_), channel_id=1, source_target_pairs={{0,2},{2,0},{4,6},{6,4},{8,10},{10,8},{12,14},{14,12},{16,18},{18,... | collective-permute-start | bytes 2457608 | tf_op jit(solution)/shard_map/ppermute | solution.py:305
  77.5 21.8 %collective-permute-start.11 = (bf16[3,128,1024]{2,1,0:T(8,128)(2,1)S(1)}, bf16[3,128,1024]{2,1,0:T(8,128)(2,1)S(1)}, u32[]{:S(2)}, u32[]{:S(2)}) collective-permute-start(bf16[3,128,1024]{2,1,0:T(8,128)(2,1)S(1)} %pad_maximum_fusion), channel_id=1, source_target_pairs={{0,1},{1,0},{2,3},{3,2},{4,5},{5,4},{6,7},{7,6},{8,9},{9,8},{10,11... | collective-permute-start | bytes 2359304 | tf_op jit(solution)/shard_map/ppermute | solution.py:316
  113.1 25.3 %collective-permute-start.25 = (bf16[4,128,1024]{2,1,0:T(8,128)(2,1)S(1)}, bf16[4,128,1024]{2,1,0:T(8,128)(2,1)S(1)}, u32[]{:S(2)}, u32[]{:S(2)}) collective-permute-start(bf16[4,128,1024]{2,1,0:T(8,128)(2,1)S(1)} %get-tuple-element.165), channel_id=1, source_target_pairs={{0,1},{1,0},{2,3},{3,2},{4,5},{5,4},{6,7},{7,6},{8,9},{9,8},{10,11... | collective-permute-start | bytes 3145736 | tf_op jit(solution)/shard_map/ppermute | solution.py:316
  113.7 24.9 %collective-permute-start.26 = (bf16[4,128,1024]{2,1,0:T(8,128)(2,1)S(1)}, bf16[4,128,1024]{2,1,0:T(8,128)(2,1)S(1)}, u32[]{:S(2)}, u32[]{:S(2)}) collective-permute-start(bf16[4,128,1024]{2,1,0:T(8,128)(2,1)S(1)} %get-tuple-element.164), channel_id=1, source_target_pairs={{0,4},{2,6},{4,0},{6,2},{8,12},{10,14},{12,8},{14,10},{16,20},{18,... | collective-permute-start | bytes 3145736 | tf_op jit(solution)/shard_map/ppermute | solution.py:305
  138.6 21.9 %collective-permute-start.33 = (bf16[8,128,1024]{2,1,0:T(8,128)(2,1)}, bf16[8,128,1024]{2,1,0:T(8,128)(2,1)S(1)}, u32[]{:S(2)}, u32[]{:S(2)}) collective-permute-start(bf16[8,128,1024]{2,1,0:T(8,128)(2,1)} %get-tuple-element.130), channel_id=1, source_target_pairs={{0,2},{2,0},{4,6},{6,4},{8,10},{10,8},{12,14},{14,12},{16,18},{18,... | collective-permute-start | bytes 6291464 | tf_op jit(solution)/shard_map/ppermute | solution.py:305
  142.0 15.0 %collective-permute-start.31 = (bf16[2,128,1024]{2,1,0:T(8,128)(2,1)}, bf16[2,128,1024]{2,1,0:T(8,128)(2,1)S(1)}, u32[]{:S(2)}, u32[]{:S(2)}) collective-permute-start(bf16[2,128,1024]{2,1,0:T(8,128)(2,1)} %get-tuple-element.163), channel_id=1, source_target_pairs={{0,4},{2,6},{4,0},{6,2},{8,12},{10,14},{12,8},{14,10},{16,20},{18,... | collective-permute-start | bytes 1572872 | tf_op jit(solution)/shard_map/ppermute | solution.py:305
  143.5 15.0 %collective-permute-start.32 = (bf16[2,128,1024]{2,1,0:T(8,128)(2,1)}, bf16[2,128,1024]{2,1,0:T(8,128)(2,1)S(1)}, u32[]{:S(2)}, u32[]{:S(2)}) collective-permute-start(bf16[2,128,1024]{2,1,0:T(8,128)(2,1)} %get-tuple-element.162), channel_id=1, source_target_pairs={{0,1},{1,0},{2,3},{3,2},{4,5},{5,4},{6,7},{7,6},{8,9},{9,8},{10,11... | collective-permute-start | bytes 1572872 | tf_op jit(solution)/shard_map/ppermute | solution.py:316
  148.4 21.4 %collective-permute-start.29 = (bf16[2,128,1024]{2,1,0:T(8,128)(2,1)S(1)}, bf16[2,128,1024]{2,1,0:T(8,128)(2,1)S(1)}, u32[]{:S(2)}, u32[]{:S(2)}) collective-permute-start(bf16[2,128,1024]{2,1,0:T(8,128)(2,1)S(1)} %get-tuple-element.177), channel_id=1, source_target_pairs={{0,1},{1,0},{2,3},{3,2},{4,5},{5,4},{6,7},{7,6},{8,9},{9,8},{10,11... | collective-permute-start | bytes 1572872 | tf_op jit(solution)/shard_map/ppermute | solution.py:316
  149.7 20.1 %collective-permute-start.30 = (bf16[2,128,1024]{2,1,0:T(8,128)(2,1)S(1)}, bf16[2,128,1024]{2,1,0:T(8,128)(2,1)S(1)}, u32[]{:S(2)}, u32[]{:S(2)}) collective-permute-start(bf16[2,128,1024]{2,1,0:T(8,128)(2,1)S(1)} %get-tuple-element.176), channel_id=1, source_target_pairs={{0,4},{2,6},{4,0},{6,2},{8,12},{10,14},{12,8},{14,10},{16,20},{18,... | collective-permute-start | bytes 1572872 | tf_op jit(solution)/shard_map/ppermute | solution.py:305
  160.9 20.1 %collective-permute-start.34 = (bf16[2,128,1024]{2,1,0:T(8,128)(2,1)S(1)}, bf16[2,128,1024]{2,1,0:T(8,128)(2,1)S(1)}, u32[]{:S(2)}, u32[]{:S(2)}) collective-permute-start(bf16[2,128,1024]{2,1,0:T(8,128)(2,1)S(1)} %get-tuple-element.175), channel_id=1, source_target_pairs={{0,1},{1,0},{2,3},{3,2},{4,5},{5,4},{6,7},{7,6},{8,9},{9,8},{10,11... | collective-permute-start | bytes 1572872 | tf_op jit(solution)/shard_map/ppermute | solution.py:316
  162.5 18.5 %collective-permute-start.35 = (bf16[2,128,1024]{2,1,0:T(8,128)(2,1)S(1)}, bf16[2,128,1024]{2,1,0:T(8,128)(2,1)S(1)}, u32[]{:S(2)}, u32[]{:S(2)}) collective-permute-start(bf16[2,128,1024]{2,1,0:T(8,128)(2,1)S(1)} %get-tuple-element.174), channel_id=1, source_target_pairs={{0,4},{2,6},{4,0},{6,2},{8,12},{10,14},{12,8},{14,10},{16,20},{18,... | collective-permute-start | bytes 1572872 | tf_op jit(solution)/shard_map/ppermute | solution.py:305
  169.8 15.6 %collective-permute-start.38 = (bf16[2,128,1024]{2,1,0:T(8,128)(2,1)S(1)}, bf16[2,128,1024]{2,1,0:T(8,128)(2,1)S(1)}, u32[]{:S(2)}, u32[]{:S(2)}) collective-permute-start(bf16[2,128,1024]{2,1,0:T(8,128)(2,1)S(1)} %pad_maximum_fusion.3), channel_id=1, source_target_pairs={{0,8},{2,10},{4,12},{6,14},{8,0},{10,2},{12,4},{14,6},{16,24},{18,... | collective-permute-start | bytes 1572872 | tf_op jit(solution)/shard_map/ppermute | solution.py:305
  171.2 12.9 %collective-permute-start.36 = (bf16[128,1024]{1,0:T(8,128)(2,1)S(1)}, bf16[128,1024]{1,0:T(8,128)(2,1)S(1)}, u32[]{:S(2)}, u32[]{:S(2)}) collective-permute-start(bf16[128,1024]{1,0:T(8,128)(2,1)S(1)} %get-tuple-element.173), channel_id=1, source_target_pairs={{0,4},{2,6},{4,0},{6,2},{8,12},{10,14},{12,8},{14,10},{16,20},{18,... | collective-permute-start | bytes 786440 | tf_op jit(solution)/shard_map/ppermute | solution.py:305
  171.8 13.5 %collective-permute-start.37 = (bf16[128,1024]{1,0:T(8,128)(2,1)S(1)}, bf16[128,1024]{1,0:T(8,128)(2,1)S(1)}, u32[]{:S(2)}, u32[]{:S(2)}) collective-permute-start(bf16[128,1024]{1,0:T(8,128)(2,1)S(1)} %get-tuple-element.172), channel_id=1, source_target_pairs={{0,1},{1,0},{2,3},{3,2},{4,5},{5,4},{6,7},{7,6},{8,9},{9,8},{10,11... | collective-permute-start | bytes 786440 | tf_op jit(solution)/shard_map/ppermute | solution.py:316
  187.0 13.6 %collective-permute-start.41 = (bf16[2,128,1024]{2,1,0:T(8,128)(2,1)S(1)}, bf16[2,128,1024]{2,1,0:T(8,128)(2,1)S(1)}, u32[]{:S(2)}, u32[]{:S(2)}) collective-permute-start(bf16[2,128,1024]{2,1,0:T(8,128)(2,1)S(1)} %pad_maximum_fusion.4), channel_id=1, source_target_pairs={{0,8},{2,10},{4,12},{6,14},{24,16},{26,18},{28,20},{30,22},{8,24},... | collective-permute-start | bytes 1572872 | tf_op jit(solution)/shard_map/ppermute | solution.py:305
  187.3 13.2 %collective-permute-start.39 = (bf16[128,1024]{1,0:T(8,128)(2,1)S(1)}, bf16[128,1024]{1,0:T(8,128)(2,1)S(1)}, u32[]{:S(2)}, u32[]{:S(2)}) collective-permute-start(bf16[128,1024]{1,0:T(8,128)(2,1)S(1)} %get-tuple-element.171), channel_id=1, source_target_pairs={{0,4},{2,6},{4,0},{6,2},{8,12},{10,14},{12,8},{14,10},{16,20},{18,... | collective-permute-start | bytes 786440 | tf_op jit(solution)/shard_map/ppermute | solution.py:305
  187.9 12.6 %collective-permute-start.40 = (bf16[128,1024]{1,0:T(8,128)(2,1)S(1)}, bf16[128,1024]{1,0:T(8,128)(2,1)S(1)}, u32[]{:S(2)}, u32[]{:S(2)}) collective-permute-start(bf16[128,1024]{1,0:T(8,128)(2,1)S(1)} %get-tuple-element.170), channel_id=1, source_target_pairs={{0,1},{1,0},{2,3},{3,2},{4,5},{5,4},{6,7},{7,6},{8,9},{9,8},{10,11... | collective-permute-start | bytes 786440 | tf_op jit(solution)/shard_map/ppermute | solution.py:316
  201.2 27.2 %collective-permute-start.43 = (bf16[2,128,1024]{2,1,0:T(8,128)(2,1)S(1)}, bf16[2,128,1024]{2,1,0:T(8,128)(2,1)S(1)}, u32[]{:S(2)}, u32[]{:S(2)}) collective-permute-start(bf16[2,128,1024]{2,1,0:T(8,128)(2,1)S(1)} %fusion), channel_id=1, source_target_pairs={{8,16},{10,18},{12,20},{14,22},{16,8},{18,10},{20,12},{22,14},{9,1... | collective-permute-start | bytes 1572872 | tf_op jit(solution)/shard_map/ppermute | solution.py:305
  204.0 24.3 %collective-permute-start.42 = (bf16[2,128,1024]{2,1,0:T(8,128)(2,1)S(1)}, bf16[2,128,1024]{2,1,0:T(8,128)(2,1)S(1)}, u32[]{:S(2)}, u32[]{:S(2)}) collective-permute-start(bf16[2,128,1024]{2,1,0:T(8,128)(2,1)S(1)} %pad_maximum_fusion.5), channel_id=1, source_target_pairs={{0,24},{2,26},{4,28},{6,30},{24,0},{26,2},{28,4},{30,6},{1,25},{3,... | collective-permute-start | bytes 1572872 | tf_op jit(solution)/shard_map/ppermute | solution.py:305
  (29 other events, 293.0 us)
